TPU v7x, 32 devices: a whole 2x2x4 slice. The times are simulated.
32 devices in a mesh: elem: 8 (over z, x), band: 4 (over y, core).
Axes of the slice: x: 2, y: 2, z: 4, core: 2. Of those that a mesh axis runs over, the one named last changes fastest.
Arguments:
- basis_counts: int32 [64, 16], P('elem', 'band'), may hold values from 1 to 128, as said below
- neighbour_codes: int32 [64, 16, 6], P('elem', 'band'), may hold values from 0 to 8, as said below
- x_block: bfloat16 [64, 16, 160, 128], P('elem', 'band'), may hold values from -6 to 6
- h_self: bfloat16 [64, 16, 128, 128], P('elem', 'band'), may hold values from -0.375 to 0.375
- h_near: bfloat16 [64, 16, 6, 128, 128], P('elem', 'band'), may hold values from -0.375 to 0.375
Outputs:
- filtered: bfloat16 [64, 16, 160, 128], P('elem', 'band')
- gram: float32 [160, 160], P('band')
- ritz: float32 [160, 160], P('band')
Inputs may be any that keep to these rules, and one draw needn't show every extreme that they name: `basis_counts`: at least one element holds exactly 128 basis functions. `neighbour_codes`: an element's 6 codes are distinct and never 4; code q names the element offset by q // 3 - 1 along the first dimension and q % 3 - 1 along the second, periodically.
All inputs are finite; a program needn't handle non-finite values.
Results may differ from a plain program's by a relative error of at most 0.007.
Values may be sent and summed in bfloat16 or wider, within the bound.
A program may use at most 128 MiB of HBM per device.

v0:
```python
import jax
import jax.numpy as jnp
from jax import lax
from jax.sharding import PartitionSpec as P

cheb_center = 0.25
cheb_half = 1.5


def extended_2(block, sides, width):
    for axis, dim in sides:
        count = lax.axis_size(axis)
        forward = [(i, i + 1) for i in range(count - 1)]
        forward.append((count - 1, 0))
        backward = [(target, source) for source, target in forward]
        low = lax.ppermute(
            lax.slice_in_dim(block, block.shape[dim] - width, None, axis=dim), axis, forward
        )
        high = lax.ppermute(lax.slice_in_dim(block, 0, width, axis=dim), axis, backward)
        block = jnp.concatenate([low, block, high], axis=dim)
    return block


def on_device(basis_counts, neighbour_codes, x_block, h_self, h_near):
    elem_rows, elem_cols, columns, basis_max = x_block.shape
    neighbours = neighbour_codes.shape[2]
    elements = elem_rows * elem_cols
    width_ext = elem_cols + 2
    live_mask = (
        lax.broadcasted_iota(jnp.int32, (elem_rows, elem_cols, 1, basis_max), 3)
        < basis_counts[:, :, None, None]
    )
    row_iota = lax.broadcasted_iota(jnp.int32, (elem_rows, elem_cols, neighbours), 0)
    col_iota = lax.broadcasted_iota(jnp.int32, (elem_rows, elem_cols, neighbours), 1)
    gather_index = (
        (row_iota + neighbour_codes // 3) * width_ext + col_iota + neighbour_codes % 3
    ).reshape(elements, neighbours)
    self_flat = h_self.reshape(elements, basis_max, basis_max)
    near_flat = h_near.reshape(elements, neighbours, basis_max, basis_max)

    def expand(vector_block):
        return extended_2(vector_block, (("elem", 0), ("band", 1)), 1)

    def apply_op(vector_block):
        extended = expand(vector_block).reshape((elem_rows + 2) * width_ext, columns, basis_max)
        nearby = jnp.take(extended, gather_index, axis=0)
        summed = jnp.einsum(
            "ecs,esr->ecr",
            vector_block.reshape(elements, columns, basis_max),
            self_flat,
            preferred_element_type=jnp.float32,
        )
        summed = summed + jnp.einsum(
            "ekcs,eksr->ecr", nearby, near_flat, preferred_element_type=jnp.float32
        )
        summed = summed.reshape(elem_rows, elem_cols, columns, basis_max)
        return jnp.where(live_mask, summed, jnp.float32(0.0))

    start = jnp.where(live_mask, x_block, jnp.zeros_like(x_block))
    first = ((apply_op(start) - cheb_center * start.astype(jnp.float32)) / cheb_half).astype(
        jnp.bfloat16
    )
    second = (
        2.0 * (apply_op(first) - cheb_center * first.astype(jnp.float32)) / cheb_half
        - start.astype(jnp.float32)
    ).astype(jnp.bfloat16)
    filtered = (
        2.0 * (apply_op(second) - cheb_center * second.astype(jnp.float32)) / cheb_half
        - first.astype(jnp.float32)
    ).astype(jnp.bfloat16)
    image = apply_op(filtered).astype(jnp.bfloat16)
    filt_flat = filtered.reshape(elements, columns, basis_max)
    gram_part = jnp.einsum("ecr,edr->cd", filt_flat, filt_flat, preferred_element_type=jnp.float32)
    ritz_part = jnp.einsum(
        "ecr,edr->cd",
        filt_flat,
        image.reshape(elements, columns, basis_max),
        preferred_element_type=jnp.float32,
    )
    band_count = lax.axis_size("band")
    normalizer = jnp.float32(elements * lax.axis_size("elem") * band_count * basis_max / 3.0)
    gram_share, ritz_share = (
        lax.psum_scatter(
            gram_part.astype(jnp.bfloat16), "band", scatter_dimension=0, tiled=True
        ).astype(jnp.float32),
        lax.psum_scatter(
            ritz_part.astype(jnp.bfloat16), "band", scatter_dimension=0, tiled=True
        ).astype(jnp.float32),
    )
    gram_rows, ritz_rows = lax.psum((gram_share, ritz_share), "elem")
    return (filtered, gram_rows / normalizer, ritz_rows / normalizer)


def solution(mesh):
    in_specs = (
        P("elem", "band"),
        P("elem", "band", None),
        P("elem", "band", None, None),
        P("elem", "band", None, None),
        P("elem", "band", None, None, None),
    )
    out_specs = (P("elem", "band", None, None), P("band", None), P("band", None))
    return jax.shard_map(
        on_device, mesh=mesh, in_specs=in_specs, out_specs=out_specs, check_vma=False
    )
```

profile of v0, /device:TPU:0, one launch (start us, length us, event | category | flops | bytes accessed | tf_op | source)
XLA Modules:
  0.0 248.6 jit_solution(6527252231957612786)
XLA Ops:
  9.6 3.0 %collective-permute-start = (bf16[1,4,160,128]{3,2,1,0:T(8,128)(2,1)S(1)}, bf16[1,4,160,128]{3,2,1,0:T(8,128)(2,1)S(1)}, u32[]{:S(2)}, u32[]{:S(2)}) collective-permute-start(bf16[1,4,160,128]{3,2,1,0:T(8,128)(2,1)S(1)} %get-tuple-element.20), channel_id=1, source_target_pairs={{0,4},{4,8},{8,12},{12,16},{16,20},{20,24},{24,28},{28,0},{1,5},{5... | collective-permute-start | bytes 491528 | tf_op jit(solution)/shard_map/ppermute | solution.py:16
  12.6 3.1 %collective-permute-start.1 = (bf16[1,4,160,128]{3,2,1,0:T(8,128)(2,1)S(1)}, bf16[1,4,160,128]{3,2,1,0:T(8,128)(2,1)S(1)}, u32[]{:S(2)}, u32[]{:S(2)}) collective-permute-start(bf16[1,4,160,128]{3,2,1,0:T(8,128)(2,1)S(1)} %get-tuple-element.21), channel_id=1, source_target_pairs={{4,0},{8,4},{12,8},{16,12},{20,16},{24,20},{28,24},{0,28},{5,1},{9... | collective-permute-start | bytes 491528 | tf_op jit(solution)/shard_map/ppermute | solution.py:19
  16.3 3.7 %collective-permute-done = bf16[1,4,160,128]{3,2,1,0:T(8,128)(2,1)S(1)} collective-permute-done((bf16[1,4,160,128]{3,2,1,0:T(8,128)(2,1)S(1)}, bf16[1,4,160,128]{3,2,1,0:T(8,128)(2,1)S(1)}, u32[]{:S(2)}, u32[]{:S(2)}) %collective-permute-start) | collective-permute-done | bytes 163872 | tf_op jit(solution)/shard_map/ppermute | solution.py:16
  25.8 6.0 %collective-permute-done.2 = bf16[10,1,160,128]{3,2,1,0:T(8,128)(2,1)S(1)} collective-permute-done((bf16[10,1,160,128]{3,2,1,0:T(8,128)(2,1)S(1)}, bf16[10,1,160,128]{3,2,1,0:T(8,128)(2,1)S(1)}, u32[]{:S(2)}, u32[]{:S(2)}) %collective-permute-start.2) | collective-permute-done | bytes 409632 | tf_op jit(solution)/shard_map/ppermute | solution.py:16
  34.4 8.9 %gather_fusion = bf16[192,160,128]{2,1,0:T(8,128)(2,1)} fusion(bf16[60,160,128]{2,1,0:T(8,128)(2,1)S(1)} %bitcast.64, s32[1024]{0:T(1024)S(1)} %pad_clamp_fusion), kind=kCustom, calls=%fused_computation.clone | custom fusion | bytes 15729408 | tf_op jit(solution)/shard_map/jit(_take)/gather | solution.py:46
  43.3 8.3 %bitcast_add_fusion.3 = f32[32,160,128]{2,1,0:T(8,128)S(1)} fusion(f32[32,160,128]{2,1,0:T(8,128)} %fusion.49, bf16[32,6,128,128]{3,2,1,0:T(8,128)(2,1)} %bitcast.78, bf16[32,6,160,128]{3,2,1,0:T(8,128)(2,1)} %bitcast.72, pred[32,6]{1,0:T(8,128)(4,1)S(1)} %copy.11), kind=kOutput, calls=%fused_computation.34 | convolution fusion | flops 1011220480 | bytes 19398848 | tf_op jit(solution)/shard_map/ekcs,eksr->ecr/dot_general | solution.py:53
  52.7 4.4 %collective-permute-start.5 = (bf16[1,4,160,128]{3,2,1,0:T(8,128)(2,1)S(1)}, bf16[1,4,160,128]{3,2,1,0:T(8,128)(2,1)S(1)}, u32[]{:S(2)}, u32[]{:S(2)}) collective-permute-start(bf16[1,4,160,128]{3,2,1,0:T(8,128)(2,1)S(1)} %get-tuple-element.19), channel_id=1, source_target_pairs={{4,0},{8,4},{12,8},{16,12},{20,16},{24,20},{28,24},{0,28},{5,1},{9... | collective-permute-start | bytes 491528 | tf_op jit(solution)/shard_map/ppermute | solution.py:19
  57.1 5.0 %collective-permute-done.4 = bf16[1,4,160,128]{3,2,1,0:T(8,128)(2,1)S(1)} collective-permute-done((bf16[1,4,160,128]{3,2,1,0:T(8,128)(2,1)S(1)}, bf16[1,4,160,128]{3,2,1,0:T(8,128)(2,1)S(1)}, u32[]{:S(2)}, u32[]{:S(2)}) %collective-permute-start.4) | collective-permute-done | bytes 163872 | tf_op jit(solution)/shard_map/ppermute | solution.py:16
  67.5 6.1 %collective-permute-done.6 = bf16[10,1,160,128]{3,2,1,0:T(8,128)(2,1)S(1)} collective-permute-done((bf16[10,1,160,128]{3,2,1,0:T(8,128)(2,1)S(1)}, bf16[10,1,160,128]{3,2,1,0:T(8,128)(2,1)S(1)}, u32[]{:S(2)}, u32[]{:S(2)}) %collective-permute-start.6) | collective-permute-done | bytes 409632 | tf_op jit(solution)/shard_map/ppermute | solution.py:16
  76.2 10.6 %gather_fusion.1 = bf16[192,160,128]{2,1,0:T(8,128)(2,1)} fusion(bf16[60,160,128]{2,1,0:T(8,128)(2,1)} %bitcast.66, s32[1024]{0:T(1024)S(1)} %pad_clamp_fusion), kind=kCustom, calls=%fused_computation.1.clone | custom fusion | bytes 15729408 | tf_op jit(solution)/shard_map/jit(_take)/gather | solution.py:46
  86.8 8.3 %bitcast_add_fusion.2 = f32[32,160,128]{2,1,0:T(8,128)S(1)} fusion(f32[32,160,128]{2,1,0:T(8,128)} %fusion.50, bf16[32,6,128,128]{3,2,1,0:T(8,128)(2,1)} %bitcast.79, bf16[32,6,160,128]{3,2,1,0:T(8,128)(2,1)} %bitcast.73, pred[32,6]{1,0:T(8,128)(4,1)S(1)} %copy.11), kind=kOutput, calls=%fused_computation.33 | convolution fusion | flops 1011220480 | bytes 19398848 | tf_op jit(solution)/shard_map/ekcs,eksr->ecr/dot_general | solution.py:53
  96.1 4.7 %collective-permute-start.9 = (bf16[1,4,160,128]{3,2,1,0:T(8,128)(2,1)S(1)}, bf16[1,4,160,128]{3,2,1,0:T(8,128)(2,1)S(1)}, u32[]{:S(2)}, u32[]{:S(2)}) collective-permute-start(bf16[1,4,160,128]{3,2,1,0:T(8,128)(2,1)S(1)} %get-tuple-element.17), channel_id=1, source_target_pairs={{4,0},{8,4},{12,8},{16,12},{20,16},{24,20},{28,24},{0,28},{5,1},{9... | collective-permute-start | bytes 491528 | tf_op jit(solution)/shard_map/ppermute | solution.py:19
  100.8 5.0 %collective-permute-done.8 = bf16[1,4,160,128]{3,2,1,0:T(8,128)(2,1)S(1)} collective-permute-done((bf16[1,4,160,128]{3,2,1,0:T(8,128)(2,1)S(1)}, bf16[1,4,160,128]{3,2,1,0:T(8,128)(2,1)S(1)}, u32[]{:S(2)}, u32[]{:S(2)}) %collective-permute-start.8) | collective-permute-done | bytes 163872 | tf_op jit(solution)/shard_map/ppermute | solution.py:16
  111.4 6.0 %collective-permute-done.10 = bf16[10,1,160,128]{3,2,1,0:T(8,128)(2,1)S(1)} collective-permute-done((bf16[10,1,160,128]{3,2,1,0:T(8,128)(2,1)S(1)}, bf16[10,1,160,128]{3,2,1,0:T(8,128)(2,1)S(1)}, u32[]{:S(2)}, u32[]{:S(2)}) %collective-permute-start.10) | collective-permute-done | bytes 409632 | tf_op jit(solution)/shard_map/ppermute | solution.py:16
  120.1 10.6 %gather_fusion.2 = bf16[192,160,128]{2,1,0:T(8,128)(2,1)} fusion(bf16[60,160,128]{2,1,0:T(8,128)(2,1)} %bitcast.67, s32[1024]{0:T(1024)S(1)} %pad_clamp_fusion), kind=kCustom, calls=%fused_computation.2.clone | custom fusion | bytes 15729408 | tf_op jit(solution)/shard_map/jit(_take)/gather | solution.py:46
  130.7 8.3 %bitcast_add_fusion.1 = f32[32,160,128]{2,1,0:T(8,128)S(1)} fusion(f32[32,160,128]{2,1,0:T(8,128)} %fusion.51, bf16[32,6,128,128]{3,2,1,0:T(8,128)(2,1)} %bitcast.80, bf16[32,6,160,128]{3,2,1,0:T(8,128)(2,1)} %bitcast.74, pred[32,6]{1,0:T(8,128)(4,1)S(1)} %copy.11), kind=kOutput, calls=%fused_computation.32 | convolution fusion | flops 1011220480 | bytes 19398848 | tf_op jit(solution)/shard_map/ekcs,eksr->ecr/dot_general | solution.py:53
  139.9 4.7 %collective-permute-start.13 = (bf16[1,4,160,128]{3,2,1,0:T(8,128)(2,1)S(1)}, bf16[1,4,160,128]{3,2,1,0:T(8,128)(2,1)S(1)}, u32[]{:S(2)}, u32[]{:S(2)}) collective-permute-start(bf16[1,4,160,128]{3,2,1,0:T(8,128)(2,1)S(1)} %get-tuple-element.15), channel_id=1, source_target_pairs={{4,0},{8,4},{12,8},{16,12},{20,16},{24,20},{28,24},{0,28},{5,1},{9... | collective-permute-start | bytes 491528 | tf_op jit(solution)/shard_map/ppermute | solution.py:19
  144.6 5.0 %collective-permute-done.12 = bf16[1,4,160,128]{3,2,1,0:T(8,128)(2,1)S(1)} collective-permute-done((bf16[1,4,160,128]{3,2,1,0:T(8,128)(2,1)S(1)}, bf16[1,4,160,128]{3,2,1,0:T(8,128)(2,1)S(1)}, u32[]{:S(2)}, u32[]{:S(2)}) %collective-permute-start.12) | collective-permute-done | bytes 163872 | tf_op jit(solution)/shard_map/ppermute | solution.py:16
  155.1 3.5 %fusion.52 = f32[32,160,128]{2,1,0:T(8,128)} fusion(bf16[32,160,128]{2,1,0:T(8,128)(2,1)} %bitcast.69, bf16[32,128,128]{2,1,0:T(8,128)(2,1)S(1)} %bitcast.62), kind=kOutput, calls=%fused_computation.85 | convolution fusion | flops 167772160 | bytes 4980736 | tf_op jit(solution)/shard_map/ecs,esr->ecr/dot_general | solution.py:47
  158.6 3.1 %collective-permute-done.14 = bf16[10,1,160,128]{3,2,1,0:T(8,128)(2,1)S(1)} collective-permute-done((bf16[10,1,160,128]{3,2,1,0:T(8,128)(2,1)S(1)}, bf16[10,1,160,128]{3,2,1,0:T(8,128)(2,1)S(1)}, u32[]{:S(2)}, u32[]{:S(2)}) %collective-permute-start.14) | collective-permute-done | bytes 409632 | tf_op jit(solution)/shard_map/ppermute | solution.py:16
  164.2 8.9 %gather_fusion.3 = bf16[192,160,128]{2,1,0:T(8,128)(2,1)} fusion(bf16[60,160,128]{2,1,0:T(8,128)(2,1)S(1)} %bitcast.65, s32[1024]{0:T(1024)S(1)} %pad_clamp_fusion), kind=kCustom, calls=%fused_computation.3.clone | custom fusion | bytes 15729408 | tf_op jit(solution)/shard_map/jit(_take)/gather | solution.py:46
  173.1 8.2 %bitcast_add_fusion = bf16[32,160,128]{2,1,0:T(8,128)(2,1)S(1)} fusion(f32[32,160,128]{2,1,0:T(8,128)} %fusion.52, bf16[32,6,128,128]{3,2,1,0:T(8,128)(2,1)} %bitcast.81, bf16[32,6,160,128]{3,2,1,0:T(8,128)(2,1)} %bitcast.71, pred[32,6]{1,0:T(8,128)(4,1)S(1)} %copy.11), kind=kOutput, calls=%fused_computation.31 | convolution fusion | flops 1011875840 | bytes 18088128 | tf_op jit(solution)/shard_map/ekcs,eksr->ecr/dot_general | solution.py:53
  182.6 20.0 %reduce-scatter.5.cloned.1.call-done = bf16[40,160]{1,0:T(8,128)(2,1)} async-done(((bf16[160,160]{1,0:T(8,128)(2,1)}), bf16[40,160]{1,0:T(8,128)(2,1)}) %reduce-scatter.5.cloned.1.call-update) | async-done | bytes 12816 | tf_op jit(solution)/shard_map/reduce_scatter | solution.py:86
  202.6 38.5 %all-reduce = (f32[40,160]{1,0:T(8,128)S(1)}, f32[40,160]{1,0:T(8,128)S(1)}) all-reduce(bf16[40,160]{1,0:T(8,128)(2,1)} %reduce-scatter.3.cloned.1.call-done, bf16[40,160]{1,0:T(8,128)(2,1)} %reduce-scatter.5.cloned.1.call-done), channel_id=1, replica_groups=mesh['elem'=8,'band'=4] {'elem'}, use_global_device_ids=true, to_apply=%region_1.3 | all-reduce | flops 12800 | bytes 76800 | tf_op jit(solution)/shard_map/psum | solution.py:90
  (87 shorter events, 40.2 us)
Async XLA Ops:
  7.2 16.5 %copy-start = (bf16[8,4,128,128]{3,2,1,0:T(8,128)(2,1)S(1)}, bf16[8,4,128,128]{3,2,1,0:T(8,128)(2,1)}, u32[]{:S(2)}) copy-start(bf16[8,4,128,128]{3,2,1,0:T(8,128)(2,1)} %param.10) | copy-start | bytes 3145732
  7.2 8.5 %copy-start.14 = (s32[8,4,6]{0,1,2:T(4,128)S(1)}, s32[8,4,6]{0,1,2:T(4,128)}, u32[]{:S(2)}) copy-start(s32[8,4,6]{0,1,2:T(4,128)} %param.8) | copy-start | bytes 2308
  7.2 175.4 %reduce-scatter.3.cloned.1.call-start = ((), (), s32[]{:S(2)}) async-start(), calls=%async_computation.2 | async-start | bytes 102400 | tf_op jit(solution)/shard_map/reduce_scatter | solution.py:83
  9.6 16.2 %copy-start.6 = (bf16[8,4,160,128]{3,2,1,0:T(8,128)(2,1)}, bf16[8,4,160,128]{3,2,1,0:T(8,128)(2,1)S(1)}, u32[]{:S(2)}) copy-start(bf16[8,4,160,128]{3,2,1,0:T(8,128)(2,1)S(1)} %broadcast_select_fusion) | copy-start | bytes 3932164
  9.6 10.3 %collective-permute-start = (bf16[1,4,160,128]{3,2,1,0:T(8,128)(2,1)S(1)}, bf16[1,4,160,128]{3,2,1,0:T(8,128)(2,1)S(1)}, u32[]{:S(2)}, u32[]{:S(2)}) collective-permute-start(bf16[1,4,160,128]{3,2,1,0:T(8,128)(2,1)S(1)} %get-tuple-element.20), channel_id=1, source_target_pairs={{0,4},{4,8},{8,12},{12,16},{16,20},{20,24},{24,28},{28,0},{1,5},{5... | collective-permute-start | bytes 491528 | tf_op jit(solution)/shard_map/ppermute | solution.py:16
  12.6 9.2 %collective-permute-start.1 = (bf16[1,4,160,128]{3,2,1,0:T(8,128)(2,1)S(1)}, bf16[1,4,160,128]{3,2,1,0:T(8,128)(2,1)S(1)}, u32[]{:S(2)}, u32[]{:S(2)}) collective-permute-start(bf16[1,4,160,128]{3,2,1,0:T(8,128)(2,1)S(1)} %get-tuple-element.21), channel_id=1, source_target_pairs={{4,0},{8,4},{12,8},{16,12},{20,16},{24,20},{28,24},{0,28},{5,1},{9... | collective-permute-start | bytes 491528 | tf_op jit(solution)/shard_map/ppermute | solution.py:19
  21.9 9.9 %collective-permute-start.2 = (bf16[10,1,160,128]{3,2,1,0:T(8,128)(2,1)S(1)}, bf16[10,1,160,128]{3,2,1,0:T(8,128)(2,1)S(1)}, u32[]{:S(2)}, u32[]{:S(2)}) collective-permute-start(bf16[10,1,160,128]{3,2,1,0:T(8,128)(2,1)S(1)} %get-tuple-element.12), channel_id=1, source_target_pairs={{0,1},{1,2},{2,3},{3,0},{4,5},{5,6},{6,7},{7,4},{8,9},{9,10},{10,1... | collective-permute-start | bytes 1228808 | tf_op jit(solution)/shard_map/ppermute | solution.py:16
  22.0 10.8 %collective-permute-start.3 = (bf16[10,1,160,128]{3,2,1,0:T(8,128)(2,1)S(1)}, bf16[10,1,160,128]{3,2,1,0:T(8,128)(2,1)S(1)}, u32[]{:S(2)}, u32[]{:S(2)}) collective-permute-start(bf16[10,1,160,128]{3,2,1,0:T(8,128)(2,1)S(1)} %get-tuple-element.13), channel_id=1, source_target_pairs={{1,0},{2,1},{3,2},{0,3},{5,4},{6,5},{7,6},{4,7},{9,8},{10,9},{11,1... | collective-permute-start | bytes 1228808 | tf_op jit(solution)/shard_map/ppermute | solution.py:19
  43.3 8.3 %copy-start.7 = (bf16[8,4,160,128]{3,2,1,0:T(8,128)(2,1)S(1)}, bf16[8,4,160,128]{3,2,1,0:T(8,128)(2,1)}, u32[]{:S(2)}) copy-start(bf16[8,4,160,128]{3,2,1,0:T(8,128)(2,1)} %param.9) | copy-start | bytes 3932164
  52.3 9.7 %collective-permute-start.4 = (bf16[1,4,160,128]{3,2,1,0:T(8,128)(2,1)S(1)}, bf16[1,4,160,128]{3,2,1,0:T(8,128)(2,1)S(1)}, u32[]{:S(2)}, u32[]{:S(2)}) collective-permute-start(bf16[1,4,160,128]{3,2,1,0:T(8,128)(2,1)S(1)} %get-tuple-element.18), channel_id=1, source_target_pairs={{0,4},{4,8},{8,12},{12,16},{16,20},{20,24},{24,28},{28,0},{1,5},{5... | collective-permute-start | bytes 491528 | tf_op jit(solution)/shard_map/ppermute | solution.py:16
  52.7 10.8 %collective-permute-start.5 = (bf16[1,4,160,128]{3,2,1,0:T(8,128)(2,1)S(1)}, bf16[1,4,160,128]{3,2,1,0:T(8,128)(2,1)S(1)}, u32[]{:S(2)}, u32[]{:S(2)}) collective-permute-start(bf16[1,4,160,128]{3,2,1,0:T(8,128)(2,1)S(1)} %get-tuple-element.19), channel_id=1, source_target_pairs={{4,0},{8,4},{12,8},{16,12},{20,16},{24,20},{28,24},{0,28},{5,1},{9... | collective-permute-start | bytes 491528 | tf_op jit(solution)/shard_map/ppermute | solution.py:19
  63.6 9.9 %collective-permute-start.6 = (bf16[10,1,160,128]{3,2,1,0:T(8,128)(2,1)S(1)}, bf16[10,1,160,128]{3,2,1,0:T(8,128)(2,1)S(1)}, u32[]{:S(2)}, u32[]{:S(2)}) collective-permute-start(bf16[10,1,160,128]{3,2,1,0:T(8,128)(2,1)S(1)} %get-tuple-element.10), channel_id=1, source_target_pairs={{0,1},{1,2},{2,3},{3,0},{4,5},{5,6},{6,7},{7,4},{8,9},{9,10},{10,1... | collective-permute-start | bytes 1228808 | tf_op jit(solution)/shard_map/ppermute | solution.py:16
  63.6 10.8 %collective-permute-start.7 = (bf16[10,1,160,128]{3,2,1,0:T(8,128)(2,1)S(1)}, bf16[10,1,160,128]{3,2,1,0:T(8,128)(2,1)S(1)}, u32[]{:S(2)}, u32[]{:S(2)}) collective-permute-start(bf16[10,1,160,128]{3,2,1,0:T(8,128)(2,1)S(1)} %get-tuple-element.11), channel_id=1, source_target_pairs={{1,0},{2,1},{3,2},{0,3},{5,4},{6,5},{7,6},{4,7},{9,8},{10,9},{11,1... | collective-permute-start | bytes 1228808 | tf_op jit(solution)/shard_map/ppermute | solution.py:19
  96.0 22.4 %copy-start.1 = (bf16[8,4,160,128]{3,2,1,0:T(8,128)(2,1)}, bf16[8,4,160,128]{3,2,1,0:T(8,128)(2,1)S(1)}, u32[]{:S(2)}) copy-start(bf16[8,4,160,128]{3,2,1,0:T(8,128)(2,1)S(1)} %fusion.19) | copy-start | bytes 3932164
  96.0 9.7 %collective-permute-start.8 = (bf16[1,4,160,128]{3,2,1,0:T(8,128)(2,1)S(1)}, bf16[1,4,160,128]{3,2,1,0:T(8,128)(2,1)S(1)}, u32[]{:S(2)}, u32[]{:S(2)}) collective-permute-start(bf16[1,4,160,128]{3,2,1,0:T(8,128)(2,1)S(1)} %get-tuple-element.16), channel_id=1, source_target_pairs={{0,4},{4,8},{8,12},{12,16},{16,20},{20,24},{24,28},{28,0},{1,5},{5... | collective-permute-start | bytes 491528 | tf_op jit(solution)/shard_map/ppermute | solution.py:16
  96.1 11.3 %collective-permute-start.9 = (bf16[1,4,160,128]{3,2,1,0:T(8,128)(2,1)S(1)}, bf16[1,4,160,128]{3,2,1,0:T(8,128)(2,1)S(1)}, u32[]{:S(2)}, u32[]{:S(2)}) collective-permute-start(bf16[1,4,160,128]{3,2,1,0:T(8,128)(2,1)S(1)} %get-tuple-element.17), channel_id=1, source_target_pairs={{4,0},{8,4},{12,8},{16,12},{20,16},{24,20},{28,24},{0,28},{5,1},{9... | collective-permute-start | bytes 491528 | tf_op jit(solution)/shard_map/ppermute | solution.py:19
  107.5 9.9 %collective-permute-start.10 = (bf16[10,1,160,128]{3,2,1,0:T(8,128)(2,1)S(1)}, bf16[10,1,160,128]{3,2,1,0:T(8,128)(2,1)S(1)}, u32[]{:S(2)}, u32[]{:S(2)}) collective-permute-start(bf16[10,1,160,128]{3,2,1,0:T(8,128)(2,1)S(1)} %get-tuple-element.8), channel_id=1, source_target_pairs={{0,1},{1,2},{2,3},{3,0},{4,5},{5,6},{6,7},{7,4},{8,9},{9,10},{10,1... | collective-permute-start | bytes 1228808 | tf_op jit(solution)/shard_map/ppermute | solution.py:16
  107.6 10.8 %collective-permute-start.11 = (bf16[10,1,160,128]{3,2,1,0:T(8,128)(2,1)S(1)}, bf16[10,1,160,128]{3,2,1,0:T(8,128)(2,1)S(1)}, u32[]{:S(2)}, u32[]{:S(2)}) collective-permute-start(bf16[10,1,160,128]{3,2,1,0:T(8,128)(2,1)S(1)} %get-tuple-element.9), channel_id=1, source_target_pairs={{1,0},{2,1},{3,2},{0,3},{5,4},{6,5},{7,6},{4,7},{9,8},{10,9},{11,1... | collective-permute-start | bytes 1228808 | tf_op jit(solution)/shard_map/ppermute | solution.py:19
  139.8 13.8 %copy-start.3 = (bf16[8,4,160,128]{3,2,1,0:T(8,128)(2,1)}, bf16[8,4,160,128]{3,2,1,0:T(8,128)(2,1)S(1)}, u32[]{:S(2)}) copy-start(bf16[8,4,160,128]{3,2,1,0:T(8,128)(2,1)S(1)} %fusion.22) | copy-start | bytes 3932164
  139.8 9.7 %collective-permute-start.12 = (bf16[1,4,160,128]{3,2,1,0:T(8,128)(2,1)S(1)}, bf16[1,4,160,128]{3,2,1,0:T(8,128)(2,1)S(1)}, u32[]{:S(2)}, u32[]{:S(2)}) collective-permute-start(bf16[1,4,160,128]{3,2,1,0:T(8,128)(2,1)S(1)} %get-tuple-element.14), channel_id=1, source_target_pairs={{0,4},{4,8},{8,12},{12,16},{16,20},{20,24},{24,28},{28,0},{1,5},{5... | collective-permute-start | bytes 491528 | tf_op jit(solution)/shard_map/ppermute | solution.py:16
  139.9 11.3 %collective-permute-start.13 = (bf16[1,4,160,128]{3,2,1,0:T(8,128)(2,1)S(1)}, bf16[1,4,160,128]{3,2,1,0:T(8,128)(2,1)S(1)}, u32[]{:S(2)}, u32[]{:S(2)}) collective-permute-start(bf16[1,4,160,128]{3,2,1,0:T(8,128)(2,1)S(1)} %get-tuple-element.15), channel_id=1, source_target_pairs={{4,0},{8,4},{12,8},{16,12},{20,16},{24,20},{28,24},{0,28},{5,1},{9... | collective-permute-start | bytes 491528 | tf_op jit(solution)/shard_map/ppermute | solution.py:19
  151.9 9.9 %collective-permute-start.14 = (bf16[10,1,160,128]{3,2,1,0:T(8,128)(2,1)S(1)}, bf16[10,1,160,128]{3,2,1,0:T(8,128)(2,1)S(1)}, u32[]{:S(2)}, u32[]{:S(2)}) collective-permute-start(bf16[10,1,160,128]{3,2,1,0:T(8,128)(2,1)S(1)} %get-tuple-element.6), channel_id=1, source_target_pairs={{0,1},{1,2},{2,3},{3,0},{4,5},{5,6},{6,7},{7,4},{8,9},{9,10},{10,1... | collective-permute-start | bytes 1228808 | tf_op jit(solution)/shard_map/ppermute | solution.py:16
  151.9 10.8 %collective-permute-start.15 = (bf16[10,1,160,128]{3,2,1,0:T(8,128)(2,1)S(1)}, bf16[10,1,160,128]{3,2,1,0:T(8,128)(2,1)}, u32[]{:S(2)}, u32[]{:S(2)}) collective-permute-start(bf16[10,1,160,128]{3,2,1,0:T(8,128)(2,1)S(1)} %get-tuple-element.7), channel_id=1, source_target_pairs={{1,0},{2,1},{3,2},{0,3},{5,4},{6,5},{7,6},{4,7},{9,8},{10,9},{11,1... | collective-permute-start | bytes 1228808 | tf_op jit(solution)/shard_map/ppermute | solution.py:19
  154.8 47.8 %reduce-scatter.5.cloned.1.call-start = ((), (), s32[]{:S(2)}) async-start(), calls=%async_computation.3 | async-start | bytes 102400 | tf_op jit(solution)/shard_map/reduce_scatter | solution.py:86
  (9 other events, 45.3 us)
Sparse Core Ops, SparseCore 0:
  154.9 18.9 reduce-scatter.2
  182.6 19.9 reduce-scatter.4
where the time goes:
time: 249 us
  waiting for transfers between devices  69.3 us (28%)
  matrix products  45.3 us (18%)
  local copies, waits for them, and re-layouts  41.9 us (17%)
  blocking collectives  38.5 us (15%)
  starting transfers between devices  27.9 us (11%)
  between operations  14.3 us (6%)
  other arithmetic  11.5 us (5%)
    ppermute x8, waiting for transfers between devices, extended_2(): lax.ppermute(lax.slice_in_dim(block, block.shape[dim] - width, None, axis...  39.8 us
    gather x4, local copies, waits for them, and re-layouts, apply_op(): nearby = jnp.take(extended, gather_index, axis=0)  39.1 us
    psum x1, blocking collectives, on_device(): gram_rows, ritz_rows = lax.psum((gram_share, ritz_share), 'elem')  38.5 us
    dot_general x4, matrix products, apply_op(): jnp.einsum('ekcs,eksr->ecr', nearby, near_flat, preferred_element_type=jn...  33.2 us
    ppermute x8, starting transfers between devices, extended_2(): lax.ppermute(lax.slice_in_dim(block, 0, width, axis=dim), axis, backward)  23.9 us
    reduce_scatter x1, waiting for transfers between devices, on_device(): lax.psum_scatter(ritz_part.astype(jnp.bfloat16), 'band', scatter_dimensio...  20 us
    dot_general x4, matrix products, apply_op(): jnp.einsum('ecs,esr->ecr', vector_block.reshape(elements, columns, basis_...  9.75 us
    ppermute x8, waiting for transfers between devices, extended_2(): lax.ppermute(lax.slice_in_dim(block, 0, width, axis=dim), axis, backward)  9.36 us
  transfers between devices with their start and end apart: 18, of which 17 were waited for; matrix products, arithmetic and copies ran while one was open for 13% of the time, Pallas kernels for 0%

commit v1 on v0

v1 whole, which is shorter than its diff:
```python
import functools

import jax
import jax.numpy as jnp
from jax import lax
from jax.experimental import pallas as pl
from jax.experimental.pallas import tpu as pltpu
from jax.sharding import PartitionSpec as P

MESH = pl.DeviceIdType.MESH
cheb_center = 0.25
cheb_half = 1.5
steps = 4
halves = 2
directions = [(a, b) for a in (-1, 0, 1) for b in (-1, 0, 1) if (a, b) != (0, 0)]


def edge(shift, count):
    if shift == 0:
        return 1, 1, count
    return (count, 0, 1) if shift > 0 else (1, count + 1, 1)


def kernel(elem_count, band_count, counts, codes, x_ref, self_ref, near_ref, out_ref, gram_ref, ritz_ref, *scratch):
    exts = [scratch[step * halves : (step + 1) * halves] for step in range(steps)]
    blocks, images, send_sem, recv_sem, load_sem, out_sem = scratch[steps * halves :]
    rows, cols, neighbours = codes.shape
    columns, basis = x_ref.shape[2:]
    part = columns // halves
    depth = near_ref.shape[2]

    my_elem, my_band = lax.axis_index("elem"), lax.axis_index("band")
    partners = [
        (lax.rem(my_elem + a + elem_count, elem_count), lax.rem(my_band + b + band_count, band_count))
        for a, b in directions
    ]

    x_loads = [
        pltpu.make_async_copy(
            x_ref.at[:, :, pl.ds(half * part, part)],
            exts[0][half].at[pl.ds(1, rows), pl.ds(1, cols)],
            load_sem.at[half],
        )
        for half in range(halves)
    ]
    h_loads = [
        pltpu.make_async_copy(near_ref, blocks.at[:, :, pl.ds(0, depth)], load_sem.at[halves]),
        pltpu.make_async_copy(self_ref, blocks.at[:, :, pl.ds(depth, basis)], load_sem.at[halves + 1]),
    ]
    for copy in x_loads + h_loads:
        copy.start()

    barrier = pltpu.get_barrier_semaphore()
    for partner in partners:
        pl.semaphore_signal(barrier, inc=1, device_id=partner, device_id_type=MESH)
    pl.semaphore_wait(barrier, len(partners))

    lanes = lax.broadcasted_iota(jnp.int32, (part, basis), 1)

    def halo(step, half, which):
        a, b = directions[which]
        row_from, row_to, row_len = edge(a, rows)
        col_from, col_to, col_len = edge(b, cols)
        ext = exts[step][half]
        return pltpu.make_async_remote_copy(
            src_ref=ext.at[pl.ds(row_from, row_len), pl.ds(col_from, col_len)],
            dst_ref=ext.at[pl.ds(row_to, row_len), pl.ds(col_to, col_len)],
            send_sem=send_sem.at[step, half, which],
            recv_sem=recv_sem.at[step, half, which],
            device_id=partners[which],
            device_id_type=MESH,
        )

    vertical = [d for d, (a, b) in enumerate(directions) if a != 0]
    sideways = [d for d, (a, b) in enumerate(directions) if a == 0]

    for half in range(halves):
        x_loads[half].wait()
        ext = exts[0][half]

        def clear(row, carry, ext=ext):
            for col in range(cols):
                held = ext[row + 1, col + 1]
                ext[row + 1, col + 1] = jnp.where(
                    lanes < counts[row, col], held.astype(jnp.float32), 0.0
                ).astype(held.dtype)
            return carry

        lax.fori_loop(0, rows, clear, 0)
        for which in sideways + vertical:
            halo(0, half, which).start()

    def one_row(step, half, row):
        ext = exts[step][half]
        for col in range(cols):
            pieces = []
            for k in range(neighbours):
                code = codes[row, col, k]
                a = (code * 11) >> 5
                pieces.append(ext[row + a, col + code - 3 * a])
            own = ext[row + 1, col + 1]
            pieces.append(own)
            summed = jnp.dot(
                jnp.concatenate(pieces, axis=1), blocks[row, col], preferred_element_type=jnp.float32
            )
            if step < steps - 1:
                value = (summed - cheb_center * own.astype(jnp.float32)) * (
                    (1.0 if step == 0 else 2.0) / cheb_half
                )
                if step > 0:
                    value = value - exts[step - 1][half][row + 1, col + 1].astype(jnp.float32)
                value = jnp.where(lanes < counts[row, col], value, 0.0)
                exts[step + 1][half][row + 1, col + 1] = value.astype(own.dtype)
            else:
                value = jnp.where(lanes < counts[row, col], summed, 0.0)
                images[row, col, pl.ds(half * part, part)] = value.astype(own.dtype)

    def row_loop(first, count, stride, step, half):
        def body(i, carry):
            one_row(step, half, first + i * stride)
            return carry

        lax.fori_loop(0, count, body, 0)

    def wide(row):
        return jnp.concatenate(
            [
                jnp.concatenate([exts[steps - 1][half][row + 1, col + 1] for half in range(halves)], axis=0)
                for col in range(cols)
            ],
            axis=1,
        )

    contract = (((1,), (1,)), ((), ()))
    out_copies = []
    for step in range(steps):
        for half in range(halves):
            for which in range(len(directions)):
                halo(step, half, which).wait()
            if step == 0 and half == 0:
                for copy in h_loads:
                    copy.wait()
            row_loop(0, 2, rows - 1, step, half)
            if step < steps - 1:
                for which in vertical:
                    halo(step + 1, half, which).start()
            row_loop(1, rows - 2, 1, step, half)
            if step < steps - 1:
                for which in sideways:
                    halo(step + 1, half, which).start()
            if step == steps - 2:
                out_copies.append(
                    pltpu.make_async_copy(
                        exts[steps - 1][half].at[pl.ds(1, rows), pl.ds(1, cols)],
                        out_ref.at[:, :, pl.ds(half * part, part)],
                        out_sem.at[half],
                    )
                )
                out_copies[-1].start()
        if step == steps - 2:
            gram_ref[...] = jnp.zeros_like(gram_ref)

            def gram_body(row, carry):
                left = wide(row)
                gram_ref[...] += lax.dot_general(left, left, contract, preferred_element_type=jnp.float32)
                return carry

            lax.fori_loop(0, rows, gram_body, 0)

    ritz_ref[...] = jnp.zeros_like(ritz_ref)

    def ritz_body(row, carry):
        right = jnp.concatenate([images[row, col] for col in range(cols)], axis=1)
        ritz_ref[...] += lax.dot_general(wide(row), right, contract, preferred_element_type=jnp.float32)
        return carry

    lax.fori_loop(0, rows, ritz_body, 0)
    for copy in out_copies:
        copy.wait()


def on_device(elem_count, band_count, basis_counts, neighbour_codes, x_block, h_self, h_near):
    rows, cols, columns, basis = x_block.shape
    neighbours = neighbour_codes.shape[2]
    near = h_near.reshape(rows, cols, neighbours * basis, basis)
    ext = pltpu.VMEM((rows + 2, cols + 2, columns // halves, basis), x_block.dtype)
    whole = pl.BlockSpec(memory_space=pltpu.VMEM)
    square = jax.ShapeDtypeStruct((columns, columns), jnp.float32)
    filtered, gram_part, ritz_part = pl.pallas_call(
        functools.partial(kernel, elem_count, band_count),
        out_shape=(jax.ShapeDtypeStruct(x_block.shape, x_block.dtype), square, square),
        in_specs=[pl.BlockSpec(memory_space=pltpu.SMEM)] * 2 + [pl.BlockSpec(memory_space=pl.ANY)] * 3,
        out_specs=(pl.BlockSpec(memory_space=pl.ANY), whole, whole),
        scratch_shapes=[ext] * (steps * halves)
        + [
            pltpu.VMEM((rows, cols, (neighbours + 1) * basis, basis), h_self.dtype),
            pltpu.VMEM((rows, cols, columns, basis), x_block.dtype),
            pltpu.SemaphoreType.DMA((steps, halves, len(directions))),
            pltpu.SemaphoreType.DMA((steps, halves, len(directions))),
            pltpu.SemaphoreType.DMA((halves + 2,)),
            pltpu.SemaphoreType.DMA((halves,)),
        ],
        compiler_params=pltpu.CompilerParams(
            collective_id=0, has_side_effects=True, vmem_limit_bytes=48 * 1024 * 1024
        ),
    )(basis_counts, neighbour_codes, x_block, h_self, near)
    normalizer = jnp.float32(rows * cols * elem_count * band_count * basis / 3.0)
    gram_share, ritz_share = (
        lax.psum_scatter(piece.astype(jnp.bfloat16), "band", scatter_dimension=0, tiled=True).astype(
            jnp.float32
        )
        for piece in (gram_part, ritz_part)
    )
    gram_rows, ritz_rows = lax.psum((gram_share, ritz_share), "elem")
    return (filtered, gram_rows / normalizer, ritz_rows / normalizer)


def solution(mesh):
    in_specs = (
        P("elem", "band"),
        P("elem", "band", None),
        P("elem", "band", None, None),
        P("elem", "band", None, None),
        P("elem", "band", None, None, None),
    )
    out_specs = (P("elem", "band", None, None), P("band", None), P("band", None))
    return jax.shard_map(
        functools.partial(on_device, mesh.shape["elem"], mesh.shape["band"]),
        mesh=mesh,
        in_specs=in_specs,
        out_specs=out_specs,
        check_vma=False,
    )
```

time: 249 us -> 158 us (0.63)
  Pallas kernels: 0 us -> 57.3 us
  matrix products: 45.3 us -> 0 us
  local copies, waits for them, and re-layouts: 41.9 us -> 5.16 us
  waiting for transfers between devices: 69.3 us -> 40.5 us
  starting transfers between devices: 27.9 us -> 0.08 us
  other arithmetic: 11.5 us -> 1.91 us
    pallas_call x0 -> x1, Pallas kernels: none -> 57.3 us  [on_device(): pl.pallas_call(functools.partial(kernel, elem_count, band_count), out_sha...]
    ppermute x16 -> x0, waiting for transfers between devices: 49.2 us -> none  [the longest x8 39.8 us: extended_2(): lax.ppermute(lax.slice_in_dim(block, block.shape[dim] - width, None, axis...]
    dot_general x10 -> x0, matrix products: 45.3 us -> none  [the longest x4 33.2 us: apply_op(): jnp.einsum('ekcs,eksr->ecr', nearby, near_flat, preferred_element_type=jn...]
    gather x4 -> x0, local copies, waits for them, and re-layouts: 39.1 us -> none  [apply_op(): nearby = jnp.take(extended, gather_index, axis=0)]
    ppermute x16 -> x0, starting transfers between devices: 27.5 us -> none  [the longest x8 23.9 us: extended_2(): lax.ppermute(lax.slice_in_dim(block, 0, width, axis=dim), axis, backward)]
    reduce_scatter x2, waiting for transfers between devices: 20.1 us -> 40.4 us  [on_device(): lax.psum_scatter(piece.astype(jnp.bfloat16), 'band', scatter_dimension=0,...]
    concatenate x4 -> x0, other arithmetic: 6.63 us -> none  [extended_2(): block = jnp.concatenate([low, block, high], axis=dim)]
    unnamed x31 -> x7, local copies, waits for them, and re-layouts: 2.22 us -> 5.16 us
  transfers between devices with their start and end apart: 18 -> 2, of which waited for: 17 -> 2; matrix products, arithmetic and copies ran while one was open for 13% -> 0% of each run, Pallas kernels for 0% -> 0%
where the time goes in v1:
time: 158 us
  Pallas kernels  57.3 us (36%)
  waiting for transfers between devices  40.5 us (26%)
  blocking collectives  38.5 us (24%)
  between operations  14.1 us (9%)
  local copies, waits for them, and re-layouts  5.16 us (3%)
  other arithmetic  1.91 us (1%)
    pallas_call x1, Pallas kernels, on_device(): pl.pallas_call(functools.partial(kernel, elem_count, band_count), out_sha...  57.3 us
    reduce_scatter x2, waiting for transfers between devices, on_device(): lax.psum_scatter(piece.astype(jnp.bfloat16), 'band', scatter_dimension=0,...  40.4 us
    psum x1, blocking collectives, on_device(): gram_rows, ritz_rows = lax.psum((gram_share, ritz_share), 'elem')  38.5 us
    unnamed x7, local copies, waits for them, and re-layouts  5.16 us
  transfers between devices with their start and end apart: 2, of which 2 were waited for; matrix products, arithmetic and copies ran while one was open for 0% of the time, Pallas kernels for 0%

profile of v1, /device:TPU:0, one launch (start us, length us, event | category | flops | bytes accessed | tf_op | source)
XLA Modules:
  0.0 157.5 jit_solution(13546495972996316065)
XLA Ops:
  7.2 0.0 reduce-scatter.3.cloned.1.call-start
  7.2 0.8 copy.9.codes
  8.0 0.8 copy.8.counts
  8.8 0.0 copy-start
  8.8 1.3 copy-done
  10.1 0.0 copy-start.1
  10.1 1.2 copy-done.1
  11.3 57.3 %shard_map.76 = (bf16[8,4,160,128]{3,2,1,0:T(8,128)(2,1)S(1)}, f32[160,160]{1,0:T(8,128)S(1)}, f32[160,160]{1,0:T(8,128)S(1)}) custom-call(s32[8,4]{1,0:T(8,128)S(1)} %copy.8.counts, s32[8,4,6]{2,1,0:T(4,128)S(1)} %copy.9.codes, bf16[8,4,160,128]{3,2,1,0:T(8,128)(2,1)S(1)} %copy-done, bf16[8,4,128,128]{3,2,1,0:T(8,128)(2,1)S(1)} %copy-done.1, ...), custom_call_target="tpu_custom_call" | custom-call | tf_op jit(solution)/shard_map/pallas_call | solution.py:189
  68.6 0.6 convert_element_type.12
  69.3 0.0 reduce-scatter.3.cloned.1.call-update
  69.3 0.0 reduce-scatter.5.cloned.1.call-start
  69.4 0.6 convert_element_type.14
  70.0 0.1 reduce-scatter.5.cloned.1.call-update
  70.1 18.4 %reduce-scatter.3.cloned.1.call-done = bf16[40,160]{1,0:T(8,128)(2,1)} async-done(((bf16[160,160]{1,0:T(8,128)(2,1)}), bf16[40,160]{1,0:T(8,128)(2,1)}) %reduce-scatter.3.cloned.1.call-update) | async-done | bytes 12816 | tf_op jit(solution)/shard_map/reduce_scatter | solution.py:209
  88.5 22.0 %reduce-scatter.5.cloned.1.call-done = bf16[40,160]{1,0:T(8,128)(2,1)} async-done(((bf16[160,160]{1,0:T(8,128)(2,1)}), bf16[40,160]{1,0:T(8,128)(2,1)}) %reduce-scatter.5.cloned.1.call-update) | async-done | bytes 12816 | tf_op jit(solution)/shard_map/reduce_scatter | solution.py:209
  110.5 38.5 %all-reduce = (f32[40,160]{1,0:T(8,128)S(1)}, f32[40,160]{1,0:T(8,128)S(1)}) all-reduce(bf16[40,160]{1,0:T(8,128)(2,1)} %reduce-scatter.3.cloned.1.call-done, bf16[40,160]{1,0:T(8,128)(2,1)} %reduce-scatter.5.cloned.1.call-done), channel_id=1, replica_groups=mesh['elem'=8,'band'=4] {'elem'}, use_global_device_ids=true, to_apply=%region_1.0 | all-reduce | flops 12800 | bytes 76800 | tf_op jit(solution)/shard_map/psum | solution.py:214
  149.0 0.6 broadcast_multiply_fusion
  149.6 1.1 copy.11
Async XLA Ops:
  7.2 81.3 %reduce-scatter.3.cloned.1.call-start = ((), (), s32[]{:S(2)}) async-start(), calls=%async_computation.2 | async-start | bytes 102400 | tf_op jit(solution)/shard_map/reduce_scatter | solution.py:209
  8.8 1.3 copy-start
  10.1 1.2 copy-start.1
  69.3 41.2 %reduce-scatter.5.cloned.1.call-start = ((), (), s32[]{:S(2)}) async-start(), calls=%async_computation.3 | async-start | bytes 102400 | tf_op jit(solution)/shard_map/reduce_scatter | solution.py:209
Sparse Core Ops, SparseCore 0:
  69.4 19.0 reduce-scatter.2
  90.9 19.5 reduce-scatter.4

commit v2 on v1

--- a/solution.py
+++ b/solution.py
@@ -21,13 +21,30 @@
     return (count, 0, 1) if shift > 0 else (1, count + 1, 1)
 
 
-def kernel(elem_count, band_count, counts, codes, x_ref, self_ref, near_ref, out_ref, gram_ref, ritz_ref, *scratch):
+def digits(count):
+    found, stride = [], 1
+    while stride < count:
+        left = count // stride
+        radix = 2 if left % 4 and left % 2 == 0 or stride == 1 and left % 2 == 0 else 4 if left % 4 == 0 else left
+        found.append((stride, radix))
+        stride *= radix
+    return found
+
+
+def kernel(elem_count, band_count, counts_ref, codes_ref, x_ref, self_ref, near_ref, out_ref, gram_ref, ritz_ref, *scratch):
     exts = [scratch[step * halves : (step + 1) * halves] for step in range(steps)]
-    blocks, images, send_sem, recv_sem, load_sem, out_sem = scratch[steps * halves :]
-    rows, cols, neighbours = codes.shape
+    (
+        blocks, images, totals, counts, codes, send_sem, recv_sem, load_sem, out_sem,
+        outgoing, sum_send, sum_recv, *stage_refs
+    ) = scratch[steps * halves :]
+    neighbours, cols, rows = codes_ref.shape
     columns, basis = x_ref.shape[2:]
     part = columns // halves
     depth = near_ref.shape[2]
+    owned = columns // band_count
+    padded = outgoing.shape[2]
+    stages = [("band", 1, band_count)] + [("elem", stride, radix) for stride, radix in digits(elem_count)]
+    arrived = [stage_refs[m * len(stages) : (m + 1) * len(stages)] for m in range(2)]
 
     my_elem, my_band = lax.axis_index("elem"), lax.axis_index("band")
     partners = [
@@ -35,6 +52,10 @@
         for a, b in directions
     ]
 
+    small_loads = [
+        pltpu.make_async_copy(counts_ref, counts, load_sem.at[halves + 2]),
+        pltpu.make_async_copy(codes_ref, codes, load_sem.at[halves + 3]),
+    ]
     x_loads = [
         pltpu.make_async_copy(
             x_ref.at[:, :, pl.ds(half * part, part)],
@@ -47,13 +68,27 @@
         pltpu.make_async_copy(near_ref, blocks.at[:, :, pl.ds(0, depth)], load_sem.at[halves]),
         pltpu.make_async_copy(self_ref, blocks.at[:, :, pl.ds(depth, basis)], load_sem.at[halves + 1]),
     ]
-    for copy in x_loads + h_loads:
+    for copy in small_loads + x_loads + h_loads:
         copy.start()
 
+    sum_partners = []
+    for axis, stride, radix in stages:
+        mine = my_band if axis == "band" else my_elem
+        digit = lax.rem(mine // stride, radix)
+        peers = []
+        for shift in range(1, radix):
+            other = lax.rem(digit + shift, radix)
+            moved = mine + (other - digit) * stride
+            peers.append((other, (my_elem, moved) if axis == "band" else (moved, my_band)))
+        sum_partners.append((digit, peers))
+
+    greeted = partners + [device for _, peers in sum_partners for _, device in peers]
     barrier = pltpu.get_barrier_semaphore()
-    for partner in partners:
+    for partner in greeted:
         pl.semaphore_signal(barrier, inc=1, device_id=partner, device_id_type=MESH)
-    pl.semaphore_wait(barrier, len(partners))
+    pl.semaphore_wait(barrier, len(greeted))
+    for copy in small_loads:
+        copy.wait()
 
     lanes = lax.broadcasted_iota(jnp.int32, (part, basis), 1)
 
@@ -74,6 +109,8 @@
     vertical = [d for d, (a, b) in enumerate(directions) if a != 0]
     sideways = [d for d, (a, b) in enumerate(directions) if a == 0]
 
+    totals[...] = jnp.zeros_like(totals)
+    outgoing[...] = jnp.zeros_like(outgoing)
     for half in range(halves):
         x_loads[half].wait()
         ext = exts[0][half]
@@ -82,7 +119,7 @@
             for col in range(cols):
                 held = ext[row + 1, col + 1]
                 ext[row + 1, col + 1] = jnp.where(
-                    lanes < counts[row, col], held.astype(jnp.float32), 0.0
+                    lanes < counts[col, row], held.astype(jnp.float32), 0.0
                 ).astype(held.dtype)
             return carry
 
@@ -95,7 +132,7 @@
         for col in range(cols):
             pieces = []
             for k in range(neighbours):
-                code = codes[row, col, k]
+                code = codes[k, col, row]
                 a = (code * 11) >> 5
                 pieces.append(ext[row + a, col + code - 3 * a])
             own = ext[row + 1, col + 1]
@@ -109,10 +146,10 @@
                 )
                 if step > 0:
                     value = value - exts[step - 1][half][row + 1, col + 1].astype(jnp.float32)
-                value = jnp.where(lanes < counts[row, col], value, 0.0)
+                value = jnp.where(lanes < counts[col, row], value, 0.0)
                 exts[step + 1][half][row + 1, col + 1] = value.astype(own.dtype)
             else:
-                value = jnp.where(lanes < counts[row, col], summed, 0.0)
+                value = jnp.where(lanes < counts[col, row], summed, 0.0)
                 images[row, col, pl.ds(half * part, part)] = value.astype(own.dtype)
 
     def row_loop(first, count, stride, step, half):
@@ -130,6 +167,46 @@
             ],
             axis=1,
         )
+
+    def sum_copy(which, stage, shift):
+        digit, peers = sum_partners[stage]
+        other, device = peers[shift]
+        landing = arrived[which][stage].at[digit]
+        return pltpu.make_async_remote_copy(
+            src_ref=outgoing.at[which, other] if stage == 0 else landing,
+            dst_ref=landing,
+            send_sem=sum_send.at[which, stage, shift],
+            recv_sem=sum_recv.at[which, stage, shift],
+            device_id=device,
+            device_id_type=MESH,
+        )
+
+    def send_stage(which, stage):
+        for shift in range(stages[stage][2] - 1):
+            sum_copy(which, stage, shift).start()
+
+    def begin_sum(which):
+        for block in range(band_count):
+            outgoing[which, block, pl.ds(0, owned)] = totals[which, pl.ds(block * owned, owned)].astype(
+                outgoing.dtype
+            )
+        send_stage(which, 0)
+        mine = sum_partners[0][0]
+        arrived[which][0][mine] = outgoing[which, mine]
+
+    def finish_stage(which, stage):
+        for shift in range(stages[stage][2] - 1):
+            sum_copy(which, stage, shift).wait()
+        ref = arrived[which][stage]
+        total = ref[0].astype(jnp.float32)
+        for slot in range(1, stages[stage][2]):
+            total = total + ref[slot].astype(jnp.float32)
+        if stage + 1 < len(stages):
+            arrived[which][stage + 1][sum_partners[stage + 1][0]] = total.astype(ref.dtype)
+            send_stage(which, stage + 1)
+        else:
+            scale = 3.0 / (rows * cols * elem_count * band_count * basis)
+            (gram_ref, ritz_ref)[which][...] = total[:owned] * scale
 
     contract = (((1,), (1,)), ((), ()))
     out_copies = []
@@ -157,24 +234,29 @@
                     )
                 )
                 out_copies[-1].start()
+            if step == steps - 1 and half < len(stages) - 1:
+                finish_stage(0, half)
         if step == steps - 2:
-            gram_ref[...] = jnp.zeros_like(gram_ref)
 
             def gram_body(row, carry):
                 left = wide(row)
-                gram_ref[...] += lax.dot_general(left, left, contract, preferred_element_type=jnp.float32)
+                totals[0] += lax.dot_general(left, left, contract, preferred_element_type=jnp.float32)
                 return carry
 
             lax.fori_loop(0, rows, gram_body, 0)
-
-    ritz_ref[...] = jnp.zeros_like(ritz_ref)
+            begin_sum(0)
 
     def ritz_body(row, carry):
         right = jnp.concatenate([images[row, col] for col in range(cols)], axis=1)
-        ritz_ref[...] += lax.dot_general(wide(row), right, contract, preferred_element_type=jnp.float32)
+        totals[1] += lax.dot_general(wide(row), right, contract, preferred_element_type=jnp.float32)
         return carry
 
     lax.fori_loop(0, rows, ritz_body, 0)
+    begin_sum(1)
+    for stage in range(min(halves, len(stages) - 1), len(stages)):
+        finish_stage(0, stage)
+    for stage in range(len(stages)):
+        finish_stage(1, stage)
     for copy in out_copies:
         copy.wait()
 
@@ -185,34 +267,37 @@
     near = h_near.reshape(rows, cols, neighbours * basis, basis)
     ext = pltpu.VMEM((rows + 2, cols + 2, columns // halves, basis), x_block.dtype)
     whole = pl.BlockSpec(memory_space=pltpu.VMEM)
-    square = jax.ShapeDtypeStruct((columns, columns), jnp.float32)
-    filtered, gram_part, ritz_part = pl.pallas_call(
+    owned = columns // band_count
+    padded = -(-owned // 16) * 16
+    share = jax.ShapeDtypeStruct((owned, columns), jnp.float32)
+    radices = [band_count] + [radix for _, radix in digits(elem_count)]
+    landing = [pltpu.VMEM((radix, padded, columns), jnp.bfloat16) for radix in radices]
+    anywhere = pl.BlockSpec(memory_space=pl.ANY)
+    return pl.pallas_call(
         functools.partial(kernel, elem_count, band_count),
-        out_shape=(jax.ShapeDtypeStruct(x_block.shape, x_block.dtype), square, square),
-        in_specs=[pl.BlockSpec(memory_space=pltpu.SMEM)] * 2 + [pl.BlockSpec(memory_space=pl.ANY)] * 3,
-        out_specs=(pl.BlockSpec(memory_space=pl.ANY), whole, whole),
+        out_shape=(jax.ShapeDtypeStruct(x_block.shape, x_block.dtype), share, share),
+        in_specs=[anywhere] * 5,
+        out_specs=(anywhere, whole, whole),
         scratch_shapes=[ext] * (steps * halves)
         + [
             pltpu.VMEM((rows, cols, (neighbours + 1) * basis, basis), h_self.dtype),
             pltpu.VMEM((rows, cols, columns, basis), x_block.dtype),
+            pltpu.VMEM((2, columns, columns), jnp.float32),
+            pltpu.SMEM((cols, rows), jnp.int32),
+            pltpu.SMEM((neighbours, cols, rows), jnp.int32),
             pltpu.SemaphoreType.DMA((steps, halves, len(directions))),
             pltpu.SemaphoreType.DMA((steps, halves, len(directions))),
-            pltpu.SemaphoreType.DMA((halves + 2,)),
+            pltpu.SemaphoreType.DMA((halves + 4,)),
             pltpu.SemaphoreType.DMA((halves,)),
-        ],
+            pltpu.VMEM((2, band_count, padded, columns), jnp.bfloat16),
+            pltpu.SemaphoreType.DMA((2, len(radices), max(radices) - 1)),
+            pltpu.SemaphoreType.DMA((2, len(radices), max(radices) - 1)),
+        ]
+        + landing * 2,
         compiler_params=pltpu.CompilerParams(
-            collective_id=0, has_side_effects=True, vmem_limit_bytes=48 * 1024 * 1024
+            collective_id=0, has_side_effects=True, vmem_limit_bytes=60 * 1024 * 1024
         ),
-    )(basis_counts, neighbour_codes, x_block, h_self, near)
-    normalizer = jnp.float32(rows * cols * elem_count * band_count * basis / 3.0)
-    gram_share, ritz_share = (
-        lax.psum_scatter(piece.astype(jnp.bfloat16), "band", scatter_dimension=0, tiled=True).astype(
-            jnp.float32
-        )
-        for piece in (gram_part, ritz_part)
-    )
-    gram_rows, ritz_rows = lax.psum((gram_share, ritz_share), "elem")
-    return (filtered, gram_rows / normalizer, ritz_rows / normalizer)
+    )(basis_counts.T, neighbour_codes.transpose(2, 1, 0), x_block, h_self, near)
 
 
 def solution(mesh):

time: 158 us -> 73.5 us (0.47)
  waiting for transfers between devices: 40.5 us -> 0 us
  blocking collectives: 38.5 us -> 0 us
  between operations: 14.1 us -> 0.66 us
  Pallas kernels: 57.3 us -> 69 us
  other arithmetic: 1.91 us -> 0 us
    reduce_scatter x2 -> x0, waiting for transfers between devices: 40.4 us -> none  [on_device(): lax.psum_scatter(piece.astype(jnp.bfloat16), 'band', scatter_dimension=0,...]
    psum x1 -> x0, blocking collectives: 38.5 us -> none  [on_device(): gram_rows, ritz_rows = lax.psum((gram_share, ritz_share), 'elem')]
    pallas_call x1, Pallas kernels: 57.3 us -> 69 us  [on_device(): pl.pallas_call(functools.partial(kernel, elem_count, band_count), out_sha...]
  transfers between devices with their start and end apart: 2 -> 0, of which waited for: 2 -> 0; matrix products, arithmetic and copies ran while one was open for 0% -> 0% of each run, Pallas kernels for 0% -> 0%
where the time goes in v2:
time: 73.5 us; the launch traced here: 73.3 us
  Pallas kernels  69 us (94%)
  local copies, waits for them, and re-layouts  3.73 us (5%)
    pallas_call x1, Pallas kernels, on_device(): pl.pallas_call(functools.partial(kernel, elem_count, band_count), out_sha...  69 us
    unnamed x7, local copies, waits for them, and re-layouts  3.73 us

profile of v2, /device:TPU:0, one launch (start us, length us, event | category | flops | bytes accessed | tf_op | source)
XLA Modules:
  0.0 73.3 jit_solution(5144485539988309592)
XLA Ops:
  0.6 69.0 %shard_map.76 = (bf16[8,4,160,128]{3,2,1,0:T(8,128)(2,1)}, f32[40,160]{1,0:T(8,128)}, f32[40,160]{1,0:T(8,128)}) custom-call(s32[4,8]{1,0:T(4,128)} %bitcast.5, s32[6,4,8]{2,1,0:T(4,128)} %bitcast.4, bf16[8,4,160,128]{3,2,1,0:T(8,128)(2,1)} %x_ref.1, bf16[8,4,128,128]{3,2,1,0:T(8,128)(2,1)} %self_ref.1, bf16[8,4,768,128]{3,2,1,0:T(8,128)(2,1)} %bitcast.3), custom_call_target="tpu_custom_call" | custom-call | tf_op jit(solution)/shard_map/pallas_call | solution.py:276
  69.6 0.0 copy-start.1
  69.6 0.0 copy-start
  69.6 2.5 %copy.11 = bf16[8,4,160,128]{3,2,1,0:T(8,128)(2,1)} copy(bf16[8,4,160,128]{3,2,1,0:T(8,128)(2,1)} %get-tuple-element.6) | data formatting | bytes 2621440
  72.1 0.0 copy-done.1
  72.1 0.6 copy.12
  72.7 0.0 copy-done
  72.7 0.6 copy.13
Async XLA Ops:
  69.6 2.5 %copy-start.1 = (f32[40,160]{1,0:T(8,128)S(1)}, f32[40,160]{1,0:T(8,128)}, u32[]{:S(2)}) copy-start(f32[40,160]{1,0:T(8,128)} %get-tuple-element.7) | copy-start | bytes 76804
  69.6 3.1 %copy-start = (f32[40,160]{1,0:T(8,128)S(1)}, f32[40,160]{1,0:T(8,128)}, u32[]{:S(2)}) copy-start(f32[40,160]{1,0:T(8,128)} %get-tuple-element.8) | copy-start | bytes 76804

commit v3 on v2

--- a/solution.py
+++ b/solution.py
@@ -12,7 +12,7 @@
 cheb_half = 1.5
 steps = 4
 halves = 2
-directions = [(a, b) for a in (-1, 0, 1) for b in (-1, 0, 1) if (a, b) != (0, 0)]
+ways = ("vertical", "far", "near", "sideways")
 
 
 def edge(shift, count):
@@ -34,7 +34,7 @@
 def kernel(elem_count, band_count, counts_ref, codes_ref, x_ref, self_ref, near_ref, out_ref, gram_ref, ritz_ref, *scratch):
     exts = [scratch[step * halves : (step + 1) * halves] for step in range(steps)]
     (
-        blocks, images, totals, counts, codes, send_sem, recv_sem, load_sem, out_sem,
+        blocks, totals, counts, codes, send_sem, recv_sem, load_sem, out_sem,
         outgoing, sum_send, sum_recv, *stage_refs
     ) = scratch[steps * halves :]
     neighbours, cols, rows = codes_ref.shape
@@ -44,13 +44,17 @@
     owned = columns // band_count
     padded = outgoing.shape[2]
     stages = [("band", 1, band_count)] + [("elem", stride, radix) for stride, radix in digits(elem_count)]
-    arrived = [stage_refs[m * len(stages) : (m + 1) * len(stages)] for m in range(2)]
+    arrived = [stage_refs[m * len(stages) : (m + 1) * len(stages)] for m in range(2 * halves)]
 
     my_elem, my_band = lax.axis_index("elem"), lax.axis_index("band")
-    partners = [
-        (lax.rem(my_elem + a + elem_count, elem_count), lax.rem(my_band + b + band_count, band_count))
-        for a, b in directions
-    ]
+    odd = lax.rem(my_band, 2)
+    inward, outward = 1 - 2 * odd, 2 * odd - 1
+    moves = [(way, shift) for way in ways for shift in (-1, 1)]
+
+    def device_at(a, b):
+        return lax.rem(my_elem + a + elem_count, elem_count), lax.rem(my_band + b + band_count, band_count)
+
+    partners = [device_at(a, b) for a in (-1, 0, 1) for b in (-1, 0, 1) if (a, b) != (0, 0)]
 
     small_loads = [
         pltpu.make_async_copy(counts_ref, counts, load_sem.at[halves + 2]),
@@ -93,21 +97,39 @@
     lanes = lax.broadcasted_iota(jnp.int32, (part, basis), 1)
 
     def halo(step, half, which):
-        a, b = directions[which]
-        row_from, row_to, row_len = edge(a, rows)
-        col_from, col_to, col_len = edge(b, cols)
+        way, shift = moves[which]
         ext = exts[step][half]
+        if way == "vertical":
+            start, landing, length = edge(shift, rows)
+            src = ext.at[pl.ds(start, length), pl.ds(1, cols)]
+            dst = ext.at[pl.ds(landing, length), pl.ds(1, cols)]
+            device = device_at(shift, 0)
+        elif way == "sideways":
+            start, landing, length = edge(shift, cols)
+            src = ext.at[pl.ds(1, rows), pl.ds(start, length)]
+            dst = ext.at[pl.ds(1, rows), pl.ds(landing, length)]
+            device = device_at(0, shift)
+        elif way == "far":
+            start, landing, length = edge(shift, rows)
+            src = ext.at[pl.ds(start, length), pl.ds(1 + odd * (cols - 1), 1)]
+            dst = ext.at[pl.ds(landing, length), pl.ds((1 - odd) * (cols + 1), 1)]
+            device = device_at(shift, outward)
+        else:
+            row = 0 if shift < 0 else rows + 1
+            src = ext.at[pl.ds(row, 1), pl.ds(cols - odd * (cols - 1), 1)]
+            dst = ext.at[pl.ds(row, 1), pl.ds(odd * (cols + 1), 1)]
+            device = device_at(0, inward)
         return pltpu.make_async_remote_copy(
-            src_ref=ext.at[pl.ds(row_from, row_len), pl.ds(col_from, col_len)],
-            dst_ref=ext.at[pl.ds(row_to, row_len), pl.ds(col_to, col_len)],
+            src_ref=src,
+            dst_ref=dst,
             send_sem=send_sem.at[step, half, which],
             recv_sem=recv_sem.at[step, half, which],
-            device_id=partners[which],
+            device_id=device,
             device_id_type=MESH,
         )
 
-    vertical = [d for d, (a, b) in enumerate(directions) if a != 0]
-    sideways = [d for d, (a, b) in enumerate(directions) if a == 0]
+    def chosen(*wanted):
+        return [index for index, (way, shift) in enumerate(moves) if way in wanted]
 
     totals[...] = jnp.zeros_like(totals)
     outgoing[...] = jnp.zeros_like(outgoing)
@@ -124,11 +146,23 @@
             return carry
 
         lax.fori_loop(0, rows, clear, 0)
-        for which in sideways + vertical:
+        for which in chosen("vertical", "far", "sideways"):
             halo(0, half, which).start()
+
+    contract = (((1,), (1,)), ((), ()))
+
+    def wide(row):
+        return jnp.concatenate(
+            [
+                jnp.concatenate([exts[steps - 1][half][row + 1, col + 1] for half in range(halves)], axis=0)
+                for col in range(cols)
+            ],
+            axis=1,
+        )
 
     def one_row(step, half, row):
         ext = exts[step][half]
+        images = []
         for col in range(cols):
             pieces = []
             for k in range(neighbours):
@@ -150,7 +184,11 @@
                 exts[step + 1][half][row + 1, col + 1] = value.astype(own.dtype)
             else:
                 value = jnp.where(lanes < counts[col, row], summed, 0.0)
-                images[row, col, pl.ds(half * part, part)] = value.astype(own.dtype)
+                images.append(value.astype(own.dtype))
+        if images:
+            totals[halves + half] += lax.dot_general(
+                wide(row), jnp.concatenate(images, axis=1), contract, preferred_element_type=jnp.float32
+            )
 
     def row_loop(first, count, stride, step, half):
         def body(i, carry):
@@ -158,15 +196,6 @@
             return carry
 
         lax.fori_loop(0, count, body, 0)
-
-    def wide(row):
-        return jnp.concatenate(
-            [
-                jnp.concatenate([exts[steps - 1][half][row + 1, col + 1] for half in range(halves)], axis=0)
-                for col in range(cols)
-            ],
-            axis=1,
-        )
 
     def sum_copy(which, stage, shift):
         digit, peers = sum_partners[stage]
@@ -206,24 +235,28 @@
             send_stage(which, stage + 1)
         else:
             scale = 3.0 / (rows * cols * elem_count * band_count * basis)
-            (gram_ref, ritz_ref)[which][...] = total[:owned] * scale
+            (gram_ref, ritz_ref)[which // halves][:, pl.ds(which % halves * part, part)] = total[:owned] * scale
 
     contract = (((1,), (1,)), ((), ()))
     out_copies = []
     for step in range(steps):
         for half in range(halves):
-            for which in range(len(directions)):
+            for which in chosen("vertical"):
+                halo(step, half, which).wait()
+            for which in chosen("near"):
+                halo(step, half, which).start()
+            for which in chosen("far", "sideways", "near"):
                 halo(step, half, which).wait()
             if step == 0 and half == 0:
                 for copy in h_loads:
                     copy.wait()
             row_loop(0, 2, rows - 1, step, half)
             if step < steps - 1:
-                for which in vertical:
+                for which in chosen("vertical", "far"):
                     halo(step + 1, half, which).start()
             row_loop(1, rows - 2, 1, step, half)
             if step < steps - 1:
-                for which in sideways:
+                for which in chosen("sideways"):
                     halo(step + 1, half, which).start()
             if step == steps - 2:
                 out_copies.append(
@@ -234,29 +267,28 @@
                     )
                 )
                 out_copies[-1].start()
-            if step == steps - 1 and half < len(stages) - 1:
-                finish_stage(0, half)
+            if step == steps - 1:
+                begin_sum(halves + half)
+                if half < len(stages) - 1:
+                    for which in range(halves):
+                        finish_stage(which, half)
         if step == steps - 2:
 
             def gram_body(row, carry):
                 left = wide(row)
-                totals[0] += lax.dot_general(left, left, contract, preferred_element_type=jnp.float32)
+                for half in range(halves):
+                    right = left[half * part : (half + 1) * part]
+                    totals[half] += lax.dot_general(left, right, contract, preferred_element_type=jnp.float32)
                 return carry
 
             lax.fori_loop(0, rows, gram_body, 0)
-            begin_sum(0)
-
-    def ritz_body(row, carry):
-        right = jnp.concatenate([images[row, col] for col in range(cols)], axis=1)
-        totals[1] += lax.dot_general(wide(row), right, contract, preferred_element_type=jnp.float32)
-        return carry
-
-    lax.fori_loop(0, rows, ritz_body, 0)
-    begin_sum(1)
-    for stage in range(min(halves, len(stages) - 1), len(stages)):
-        finish_stage(0, stage)
+            for half in range(halves):
+                begin_sum(half)
+
     for stage in range(len(stages)):
-        finish_stage(1, stage)
+        for which in range(2 * halves):
+            if which >= halves or stage >= min(halves, len(stages) - 1):
+                finish_stage(which, stage)
     for copy in out_copies:
         copy.wait()
 
@@ -271,7 +303,7 @@
     padded = -(-owned // 16) * 16
     share = jax.ShapeDtypeStruct((owned, columns), jnp.float32)
     radices = [band_count] + [radix for _, radix in digits(elem_count)]
-    landing = [pltpu.VMEM((radix, padded, columns), jnp.bfloat16) for radix in radices]
+    landing = [pltpu.VMEM((radix, padded, columns // halves), jnp.bfloat16) for radix in radices]
     anywhere = pl.BlockSpec(memory_space=pl.ANY)
     return pl.pallas_call(
         functools.partial(kernel, elem_count, band_count),
@@ -281,19 +313,18 @@
         scratch_shapes=[ext] * (steps * halves)
         + [
             pltpu.VMEM((rows, cols, (neighbours + 1) * basis, basis), h_self.dtype),
-            pltpu.VMEM((rows, cols, columns, basis), x_block.dtype),
-            pltpu.VMEM((2, columns, columns), jnp.float32),
+            pltpu.VMEM((2 * halves, columns, columns // halves), jnp.float32),
             pltpu.SMEM((cols, rows), jnp.int32),
             pltpu.SMEM((neighbours, cols, rows), jnp.int32),
-            pltpu.SemaphoreType.DMA((steps, halves, len(directions))),
-            pltpu.SemaphoreType.DMA((steps, halves, len(directions))),
+            pltpu.SemaphoreType.DMA((steps, halves, 2 * len(ways))),
+            pltpu.SemaphoreType.DMA((steps, halves, 2 * len(ways))),
             pltpu.SemaphoreType.DMA((halves + 4,)),
             pltpu.SemaphoreType.DMA((halves,)),
-            pltpu.VMEM((2, band_count, padded, columns), jnp.bfloat16),
-            pltpu.SemaphoreType.DMA((2, len(radices), max(radices) - 1)),
-            pltpu.SemaphoreType.DMA((2, len(radices), max(radices) - 1)),
+            pltpu.VMEM((2 * halves, band_count, padded, columns // halves), jnp.bfloat16),
+            pltpu.SemaphoreType.DMA((2 * halves, len(radices), max(radices) - 1)),
+            pltpu.SemaphoreType.DMA((2 * halves, len(radices), max(radices) - 1)),
         ]
-        + landing * 2,
+        + landing * (2 * halves),
         compiler_params=pltpu.CompilerParams(
             collective_id=0, has_side_effects=True, vmem_limit_bytes=60 * 1024 * 1024
         ),

time: 73.5 us -> 69.4 us (0.944)
  Pallas kernels: 69 us -> 64.9 us
    pallas_call x1, Pallas kernels: 69 us -> 64.9 us  [on_device(): pl.pallas_call(functools.partial(kernel, elem_count, band_count), out_sha...]
where the time goes in v3:
time: 69.4 us; the launch traced here: 69.3 us
  Pallas kernels  64.9 us (94%)
  local copies, waits for them, and re-layouts  3.73 us (5%)
    pallas_call x1, Pallas kernels, on_device(): pl.pallas_call(functools.partial(kernel, elem_count, band_count), out_sha...  64.9 us
    unnamed x7, local copies, waits for them, and re-layouts  3.73 us

profile of v3, /device:TPU:0, one launch (start us, length us, event | category | flops | bytes accessed | tf_op | source)
XLA Modules:
  0.0 69.3 jit_solution(16297884564662325872)
XLA Ops:
  0.6 64.9 %shard_map.76 = (bf16[8,4,160,128]{3,2,1,0:T(8,128)(2,1)}, f32[40,160]{1,0:T(8,128)}, f32[40,160]{1,0:T(8,128)}) custom-call(s32[4,8]{1,0:T(4,128)} %bitcast.5, s32[6,4,8]{2,1,0:T(4,128)} %bitcast.4, bf16[8,4,160,128]{3,2,1,0:T(8,128)(2,1)} %x_ref.1, bf16[8,4,128,128]{3,2,1,0:T(8,128)(2,1)} %self_ref.1, bf16[8,4,768,128]{3,2,1,0:T(8,128)(2,1)} %bitcast.3), custom_call_target="tpu_custom_call" | custom-call | tf_op jit(solution)/shard_map/pallas_call | solution.py:308
  65.5 0.0 copy-start.1
  65.5 0.0 copy-start
  65.5 2.5 %copy.11 = bf16[8,4,160,128]{3,2,1,0:T(8,128)(2,1)} copy(bf16[8,4,160,128]{3,2,1,0:T(8,128)(2,1)} %get-tuple-element.6) | data formatting | bytes 2621440
  68.0 0.0 copy-done.1
  68.0 0.6 copy.12
  68.7 0.0 copy-done
  68.7 0.6 copy.13
Async XLA Ops:
  65.5 2.5 %copy-start.1 = (f32[40,160]{1,0:T(8,128)S(1)}, f32[40,160]{1,0:T(8,128)}, u32[]{:S(2)}) copy-start(f32[40,160]{1,0:T(8,128)} %get-tuple-element.7) | copy-start | bytes 76804
  65.5 3.1 %copy-start = (f32[40,160]{1,0:T(8,128)S(1)}, f32[40,160]{1,0:T(8,128)}, u32[]{:S(2)}) copy-start(f32[40,160]{1,0:T(8,128)} %get-tuple-element.8) | copy-start | bytes 76804

commit v4 on v3

--- a/solution.py
+++ b/solution.py
@@ -34,7 +34,7 @@
 def kernel(elem_count, band_count, counts_ref, codes_ref, x_ref, self_ref, near_ref, out_ref, gram_ref, ritz_ref, *scratch):
     exts = [scratch[step * halves : (step + 1) * halves] for step in range(steps)]
     (
-        blocks, totals, counts, codes, send_sem, recv_sem, load_sem, out_sem,
+        blocks, images, totals, counts, codes, send_sem, recv_sem, load_sem, out_sem,
         outgoing, sum_send, sum_recv, *stage_refs
     ) = scratch[steps * halves :]
     neighbours, cols, rows = codes_ref.shape
@@ -160,10 +160,9 @@
             axis=1,
         )
 
-    def one_row(step, half, row):
+    def update(step, half, places):
         ext = exts[step][half]
-        images = []
-        for col in range(cols):
+        for row, col in places:
             pieces = []
             for k in range(neighbours):
                 code = codes[k, col, row]
@@ -184,18 +183,29 @@
                 exts[step + 1][half][row + 1, col + 1] = value.astype(own.dtype)
             else:
                 value = jnp.where(lanes < counts[col, row], summed, 0.0)
-                images.append(value.astype(own.dtype))
-        if images:
-            totals[halves + half] += lax.dot_general(
-                wide(row), jnp.concatenate(images, axis=1), contract, preferred_element_type=jnp.float32
-            )
-
-    def row_loop(first, count, stride, step, half):
-        def body(i, carry):
-            one_row(step, half, first + i * stride)
+                images[row, col] = value.astype(own.dtype)
+
+    def loop(count, body):
+        def run(index, carry):
+            body(index)
             return carry
 
-        lax.fori_loop(0, count, body, 0)
+        lax.fori_loop(0, count, run, 0)
+
+    group = 2 if rows % 2 == 0 else 1
+
+    def inner(step, half, wanted):
+        def body(index):
+            update(step, half, [(1 + index * group + i, col) for i in range(group) for col in wanted])
+
+        loop((rows - 2) // group, body)
+
+    def add_ritz(half):
+        def body(row):
+            right = jnp.concatenate([images[row, col] for col in range(cols)], axis=1)
+            totals[halves + half] += lax.dot_general(wide(row), right, contract, preferred_element_type=jnp.float32)
+
+        loop(rows, body)
 
     def sum_copy(which, stage, shift):
         digit, peers = sum_partners[stage]
@@ -237,7 +247,6 @@
             scale = 3.0 / (rows * cols * elem_count * band_count * basis)
             (gram_ref, ritz_ref)[which // halves][:, pl.ds(which % halves * part, part)] = total[:owned] * scale
 
-    contract = (((1,), (1,)), ((), ()))
     out_copies = []
     for step in range(steps):
         for half in range(halves):
@@ -250,14 +259,15 @@
             if step == 0 and half == 0:
                 for copy in h_loads:
                     copy.wait()
-            row_loop(0, 2, rows - 1, step, half)
+            update(step, half, [(row, col) for row in (0, rows - 1) for col in range(cols)])
             if step < steps - 1:
                 for which in chosen("vertical", "far"):
                     halo(step + 1, half, which).start()
-            row_loop(1, rows - 2, 1, step, half)
+            inner(step, half, (0, cols - 1))
             if step < steps - 1:
                 for which in chosen("sideways"):
                     halo(step + 1, half, which).start()
+            inner(step, half, range(1, cols - 1))
             if step == steps - 2:
                 out_copies.append(
                     pltpu.make_async_copy(
@@ -268,6 +278,7 @@
                 )
                 out_copies[-1].start()
             if step == steps - 1:
+                add_ritz(half)
                 begin_sum(halves + half)
                 if half < len(stages) - 1:
                     for which in range(halves):
@@ -290,6 +301,21 @@
             if which >= halves or stage >= min(halves, len(stages) - 1):
                 finish_stage(which, stage)
     for copy in out_copies:
+        copy.wait()
+
+
+def hand_on(*refs):
+    count = len(refs) // 2
+    copies = []
+    for index, (source, target) in enumerate(zip(refs[:count], refs[count:-1])):
+        if len(source.shape) == 2:
+            copies.append((source, target))
+        else:
+            copies.extend((source.at[row], target.at[row]) for row in range(source.shape[0]))
+    started = [pltpu.make_async_copy(*pair, refs[-1].at[i]) for i, pair in enumerate(copies)]
+    for copy in started:
+        copy.start()
+    for copy in started:
         copy.wait()
 
 
@@ -305,7 +331,7 @@
     radices = [band_count] + [radix for _, radix in digits(elem_count)]
     landing = [pltpu.VMEM((radix, padded, columns // halves), jnp.bfloat16) for radix in radices]
     anywhere = pl.BlockSpec(memory_space=pl.ANY)
-    return pl.pallas_call(
+    results = pl.pallas_call(
         functools.partial(kernel, elem_count, band_count),
         out_shape=(jax.ShapeDtypeStruct(x_block.shape, x_block.dtype), share, share),
         in_specs=[anywhere] * 5,
@@ -313,6 +339,7 @@
         scratch_shapes=[ext] * (steps * halves)
         + [
             pltpu.VMEM((rows, cols, (neighbours + 1) * basis, basis), h_self.dtype),
+            pltpu.VMEM((rows, cols, columns // halves, basis), x_block.dtype),
             pltpu.VMEM((2 * halves, columns, columns // halves), jnp.float32),
             pltpu.SMEM((cols, rows), jnp.int32),
             pltpu.SMEM((neighbours, cols, rows), jnp.int32),
@@ -329,6 +356,14 @@
             collective_id=0, has_side_effects=True, vmem_limit_bytes=60 * 1024 * 1024
         ),
     )(basis_counts.T, neighbour_codes.transpose(2, 1, 0), x_block, h_self, near)
+    return pl.pallas_call(
+        hand_on,
+        out_shape=tuple(jax.ShapeDtypeStruct(result.shape, result.dtype) for result in results),
+        in_specs=[anywhere] * len(results),
+        out_specs=(anywhere,) * len(results),
+        scratch_shapes=[pltpu.SemaphoreType.DMA((rows + 2,))],
+        compiler_params=pltpu.CompilerParams(vmem_limit_bytes=60 * 1024 * 1024),
+    )(*results)
 
 
 def solution(mesh):

time: 69.4 us -> 108 us (1.56)
  Pallas kernels: 64.9 us -> 107 us
  local copies, waits for them, and re-layouts: 3.73 us -> 0 us
    pallas_call x0 -> x1, Pallas kernels: none -> 43.4 us  [on_device(): pl.pallas_call(hand_on, out_shape=tuple((jax.ShapeDtypeStruct(result.shap...]
    unnamed x7 -> x0, local copies, waits for them, and re-layouts: 3.73 us -> none
where the time goes in v4:
time: 108 us
  Pallas kernels  107 us (99%)
    pallas_call x1, Pallas kernels, on_device(): pl.pallas_call(functools.partial(kernel, elem_count, band_count), out_sha...  63.8 us
    pallas_call x1, Pallas kernels, on_device(): pl.pallas_call(hand_on, out_shape=tuple((jax.ShapeDtypeStruct(result.shap...  43.4 us

profile of v4, /device:TPU:0, one launch (start us, length us, event | category | flops | bytes accessed | tf_op | source)
XLA Modules:
  0.0 107.9 jit_solution(18056857336498309359)
XLA Ops:
  0.6 63.8 %shard_map.76 = (bf16[8,4,160,128]{3,2,1,0:T(8,128)(2,1)}, f32[40,160]{1,0:T(8,128)}, f32[40,160]{1,0:T(8,128)}) custom-call(s32[4,8]{1,0:T(4,128)} %bitcast.5, s32[6,4,8]{2,1,0:T(4,128)} %bitcast.4, bf16[8,4,160,128]{3,2,1,0:T(8,128)(2,1)} %x_ref.1, bf16[8,4,128,128]{3,2,1,0:T(8,128)(2,1)} %self_ref.1, bf16[8,4,768,128]{3,2,1,0:T(8,128)(2,1)} %bitcast.3), custom_call_target="tpu_custom_call" | custom-call | tf_op jit(solution)/shard_map/pallas_call | solution.py:334
  64.5 43.4 %shard_map.77 = (bf16[8,4,160,128]{3,2,1,0:T(8,128)(2,1)}, f32[40,160]{1,0:T(8,128)}, f32[40,160]{1,0:T(8,128)}) custom-call(bf16[8,4,160,128]{3,2,1,0:T(8,128)(2,1)} %get-tuple-element.6.refs_0_, f32[40,160]{1,0:T(8,128)} %get-tuple-element.7.refs_1_, f32[40,160]{1,0:T(8,128)} %get-tuple-element.8.refs_2_), custom_call_target="tpu_custom_call" | custom-call | tf_op jit(solution)/shard_map/pallas_call | solution.py:359

commit v5 on v4

--- a/solution.py
+++ b/solution.py
@@ -162,6 +162,7 @@
 
     def update(step, half, places):
         ext = exts[step][half]
+        made = []
         for row, col in places:
             pieces = []
             for k in range(neighbours):
@@ -180,10 +181,14 @@
                 if step > 0:
                     value = value - exts[step - 1][half][row + 1, col + 1].astype(jnp.float32)
                 value = jnp.where(lanes < counts[col, row], value, 0.0)
-                exts[step + 1][half][row + 1, col + 1] = value.astype(own.dtype)
             else:
                 value = jnp.where(lanes < counts[col, row], summed, 0.0)
-                images[row, col] = value.astype(own.dtype)
+            made.append(value.astype(own.dtype))
+        for (row, col), value in zip(places, made):
+            if step < steps - 1:
+                exts[step + 1][half][row + 1, col + 1] = value
+            else:
+                images[row, col] = value
 
     def loop(count, body):
         def run(index, carry):
@@ -259,7 +264,8 @@
             if step == 0 and half == 0:
                 for copy in h_loads:
                     copy.wait()
-            update(step, half, [(row, col) for row in (0, rows - 1) for col in range(cols)])
+            for row in (0, rows - 1):
+                update(step, half, [(row, col) for col in range(cols)])
             if step < steps - 1:
                 for which in chosen("vertical", "far"):
                     halo(step + 1, half, which).start()
@@ -305,18 +311,22 @@
 
 
 def hand_on(*refs):
-    count = len(refs) // 2
+    count = (len(refs) - 1) // 3
     copies = []
-    for index, (source, target) in enumerate(zip(refs[:count], refs[count:-1])):
+    for source, target, stage in zip(refs[:count], refs[count : 2 * count], refs[2 * count : -1]):
         if len(source.shape) == 2:
-            copies.append((source, target))
+            copies.append((source, target, stage))
         else:
-            copies.extend((source.at[row], target.at[row]) for row in range(source.shape[0]))
-    started = [pltpu.make_async_copy(*pair, refs[-1].at[i]) for i, pair in enumerate(copies)]
-    for copy in started:
-        copy.start()
-    for copy in started:
-        copy.wait()
+            copies.extend((source.at[row], target.at[row], stage.at[row]) for row in range(source.shape[0]))
+    loads = [pltpu.make_async_copy(a, c, refs[-1].at[0, i]) for i, (a, b, c) in enumerate(copies)]
+    stores = [pltpu.make_async_copy(c, b, refs[-1].at[1, i]) for i, (a, b, c) in enumerate(copies)]
+    for load in loads:
+        load.start()
+    for load, store in zip(loads, stores):
+        load.wait()
+        store.start()
+    for store in stores:
+        store.wait()
 
 
 def on_device(elem_count, band_count, basis_counts, neighbour_codes, x_block, h_self, h_near):
@@ -361,7 +371,8 @@
         out_shape=tuple(jax.ShapeDtypeStruct(result.shape, result.dtype) for result in results),
         in_specs=[anywhere] * len(results),
         out_specs=(anywhere,) * len(results),
-        scratch_shapes=[pltpu.SemaphoreType.DMA((rows + 2,))],
+        scratch_shapes=[pltpu.VMEM(result.shape, result.dtype) for result in results]
+        + [pltpu.SemaphoreType.DMA((2, rows + 2))],
         compiler_params=pltpu.CompilerParams(vmem_limit_bytes=60 * 1024 * 1024),
     )(*results)
 

time: 108 us -> 66.9 us (0.62)
  Pallas kernels: 107 us -> 66.1 us
    pallas_call x1, Pallas kernels: 43.4 us -> 2.26 us  [on_device(): pl.pallas_call(hand_on, out_shape=tuple((jax.ShapeDtypeStruct(result.shap...]
where the time goes in v5:
time: 66.9 us; the launch traced here: 66.7 us
  Pallas kernels  66.1 us (99%)
    pallas_call x1, Pallas kernels, on_device(): pl.pallas_call(functools.partial(kernel, elem_count, band_count), out_sha...  63.8 us
    pallas_call x1, Pallas kernels, on_device(): pl.pallas_call(hand_on, out_shape=tuple((jax.ShapeDtypeStruct(result.shap...  2.26 us

profile of v5, /device:TPU:0, one launch (start us, length us, event | category | flops | bytes accessed | tf_op | source)
XLA Modules:
  0.0 66.7 jit_solution(5313493229900455967)
XLA Ops:
  0.6 63.8 %shard_map.76 = (bf16[8,4,160,128]{3,2,1,0:T(8,128)(2,1)}, f32[40,160]{1,0:T(8,128)}, f32[40,160]{1,0:T(8,128)}) custom-call(s32[4,8]{1,0:T(4,128)} %bitcast.5, s32[6,4,8]{2,1,0:T(4,128)} %bitcast.4, bf16[8,4,160,128]{3,2,1,0:T(8,128)(2,1)} %x_ref.1, bf16[8,4,128,128]{3,2,1,0:T(8,128)(2,1)} %self_ref.1, bf16[8,4,768,128]{3,2,1,0:T(8,128)(2,1)} %bitcast.3), custom_call_target="tpu_custom_call" | custom-call | tf_op jit(solution)/shard_map/pallas_call | solution.py:344
  64.5 2.3 %shard_map.77 = (bf16[8,4,160,128]{3,2,1,0:T(8,128)(2,1)}, f32[40,160]{1,0:T(8,128)}, f32[40,160]{1,0:T(8,128)}) custom-call(bf16[8,4,160,128]{3,2,1,0:T(8,128)(2,1)} %get-tuple-element.6.refs_0_, f32[40,160]{1,0:T(8,128)} %get-tuple-element.7.refs_1_, f32[40,160]{1,0:T(8,128)} %get-tuple-element.8.refs_2_), custom_call_target="tpu_custom_call" | custom-call | tf_op jit(solution)/shard_map/pallas_call | solution.py:369

commit v6 on v5

--- a/solution.py
+++ b/solution.py
@@ -96,18 +96,20 @@
 
     lanes = lax.broadcasted_iota(jnp.int32, (part, basis), 1)
 
-    def halo(step, half, which):
+    def halo(step, half, which, piece=None):
         way, shift = moves[which]
+        first_col, some_cols = (1, cols) if piece is None else (1 + piece * (cols // pieces), cols // pieces)
+        first_row, some_rows = (1, rows) if piece is None else (1 + piece * (rows // pieces), rows // pieces)
         ext = exts[step][half]
         if way == "vertical":
             start, landing, length = edge(shift, rows)
-            src = ext.at[pl.ds(start, length), pl.ds(1, cols)]
-            dst = ext.at[pl.ds(landing, length), pl.ds(1, cols)]
+            src = ext.at[pl.ds(start, length), pl.ds(first_col, some_cols)]
+            dst = ext.at[pl.ds(landing, length), pl.ds(first_col, some_cols)]
             device = device_at(shift, 0)
         elif way == "sideways":
             start, landing, length = edge(shift, cols)
-            src = ext.at[pl.ds(1, rows), pl.ds(start, length)]
-            dst = ext.at[pl.ds(1, rows), pl.ds(landing, length)]
+            src = ext.at[pl.ds(first_row, some_rows), pl.ds(start, length)]
+            dst = ext.at[pl.ds(first_row, some_rows), pl.ds(landing, length)]
             device = device_at(0, shift)
         elif way == "far":
             start, landing, length = edge(shift, rows)
@@ -128,11 +130,19 @@
             device_id_type=MESH,
         )
 
+    pieces = cols if rows % cols == 0 else 1
+
+    def send_halo(step, half):
+        for which in chosen("far"):
+            halo(step, half, which).start()
+        for piece in range(pieces):
+            for sideways, vertical in zip(chosen("sideways"), chosen("vertical")):
+                halo(step, half, sideways, piece).start()
+                halo(step, half, vertical, piece).start()
+
     def chosen(*wanted):
         return [index for index, (way, shift) in enumerate(moves) if way in wanted]
 
-    totals[...] = jnp.zeros_like(totals)
-    outgoing[...] = jnp.zeros_like(outgoing)
     for half in range(halves):
         x_loads[half].wait()
         ext = exts[0][half]
@@ -146,8 +156,9 @@
             return carry
 
         lax.fori_loop(0, rows, clear, 0)
-        for which in chosen("vertical", "far", "sideways"):
-            halo(0, half, which).start()
+        send_halo(0, half)
+    totals[...] = jnp.zeros_like(totals)
+    outgoing[...] = jnp.zeros_like(outgoing)
 
     contract = (((1,), (1,)), ((), ()))
 
@@ -164,15 +175,15 @@
         ext = exts[step][half]
         made = []
         for row, col in places:
-            pieces = []
+            operands = []
             for k in range(neighbours):
                 code = codes[k, col, row]
                 a = (code * 11) >> 5
-                pieces.append(ext[row + a, col + code - 3 * a])
+                operands.append(ext[row + a, col + code - 3 * a])
             own = ext[row + 1, col + 1]
-            pieces.append(own)
+            operands.append(own)
             summed = jnp.dot(
-                jnp.concatenate(pieces, axis=1), blocks[row, col], preferred_element_type=jnp.float32
+                jnp.concatenate(operands, axis=1), blocks[row, col], preferred_element_type=jnp.float32
             )
             if step < steps - 1:
                 value = (summed - cheb_center * own.astype(jnp.float32)) * (
@@ -266,13 +277,9 @@
                     copy.wait()
             for row in (0, rows - 1):
                 update(step, half, [(row, col) for col in range(cols)])
-            if step < steps - 1:
-                for which in chosen("vertical", "far"):
-                    halo(step + 1, half, which).start()
             inner(step, half, (0, cols - 1))
             if step < steps - 1:
-                for which in chosen("sideways"):
-                    halo(step + 1, half, which).start()
+                send_halo(step + 1, half)
             inner(step, half, range(1, cols - 1))
             if step == steps - 2:
                 out_copies.append(

time: 66.9 us -> 72 us (1.076)
  Pallas kernels: 66.1 us -> 71.3 us
    pallas_call x1, Pallas kernels: 63.8 us -> 69 us  [on_device(): pl.pallas_call(functools.partial(kernel, elem_count, band_count), out_sha...]
where the time goes in v6:
time: 72 us; the launch traced here: 71.9 us
  Pallas kernels  71.3 us (99%)
    pallas_call x1, Pallas kernels, on_device(): pl.pallas_call(functools.partial(kernel, elem_count, band_count), out_sha...  69 us
    pallas_call x1, Pallas kernels, on_device(): pl.pallas_call(hand_on, out_shape=tuple((jax.ShapeDtypeStruct(result.shap...  2.26 us

profile of v6, /device:TPU:0, one launch (start us, length us, event | category | flops | bytes accessed | tf_op | source)
XLA Modules:
  0.0 71.9 jit_solution(5055001169002038053)
XLA Ops:
  0.6 69.0 %shard_map.76 = (bf16[8,4,160,128]{3,2,1,0:T(8,128)(2,1)}, f32[40,160]{1,0:T(8,128)}, f32[40,160]{1,0:T(8,128)}) custom-call(s32[4,8]{1,0:T(4,128)} %bitcast.5, s32[6,4,8]{2,1,0:T(4,128)} %bitcast.4, bf16[8,4,160,128]{3,2,1,0:T(8,128)(2,1)} %x_ref.1, bf16[8,4,128,128]{3,2,1,0:T(8,128)(2,1)} %self_ref.1, bf16[8,4,768,128]{3,2,1,0:T(8,128)(2,1)} %bitcast.3), custom_call_target="tpu_custom_call" | custom-call | tf_op jit(solution)/shard_map/pallas_call | solution.py:351
  69.6 2.3 %shard_map.77 = (bf16[8,4,160,128]{3,2,1,0:T(8,128)(2,1)}, f32[40,160]{1,0:T(8,128)}, f32[40,160]{1,0:T(8,128)}) custom-call(bf16[8,4,160,128]{3,2,1,0:T(8,128)(2,1)} %get-tuple-element.6.refs_0_, f32[40,160]{1,0:T(8,128)} %get-tuple-element.7.refs_1_, f32[40,160]{1,0:T(8,128)} %get-tuple-element.8.refs_2_), custom_call_target="tpu_custom_call" | custom-call | tf_op jit(solution)/shard_map/pallas_call | solution.py:376

commit v7 on v5

--- a/solution.py
+++ b/solution.py
@@ -131,8 +131,6 @@
     def chosen(*wanted):
         return [index for index, (way, shift) in enumerate(moves) if way in wanted]
 
-    totals[...] = jnp.zeros_like(totals)
-    outgoing[...] = jnp.zeros_like(outgoing)
     for half in range(halves):
         x_loads[half].wait()
         ext = exts[0][half]
@@ -148,6 +146,8 @@
         lax.fori_loop(0, rows, clear, 0)
         for which in chosen("vertical", "far", "sideways"):
             halo(0, half, which).start()
+    totals[...] = jnp.zeros_like(totals)
+    outgoing[...] = jnp.zeros_like(outgoing)
 
     contract = (((1,), (1,)), ((), ()))
 
@@ -252,13 +252,16 @@
             scale = 3.0 / (rows * cols * elem_count * band_count * basis)
             (gram_ref, ritz_ref)[which // halves][:, pl.ds(which % halves * part, part)] = total[:owned] * scale
 
+    def forward_corners(step, half):
+        for which in chosen("vertical"):
+            halo(step, half, which).wait()
+        for which in chosen("near"):
+            halo(step, half, which).start()
+
     out_copies = []
+    forward_corners(0, 0)
     for step in range(steps):
         for half in range(halves):
-            for which in chosen("vertical"):
-                halo(step, half, which).wait()
-            for which in chosen("near"):
-                halo(step, half, which).start()
             for which in chosen("far", "sideways", "near"):
                 halo(step, half, which).wait()
             if step == 0 and half == 0:
@@ -273,6 +276,10 @@
             if step < steps - 1:
                 for which in chosen("sideways"):
                     halo(step + 1, half, which).start()
+            if half + 1 < halves:
+                forward_corners(step, half + 1)
+            elif step < steps - 1:
+                forward_corners(step + 1, 0)
             inner(step, half, range(1, cols - 1))
             if step == steps - 2:
                 out_copies.append(

time: 66.9 us -> 69.7 us (1.042)
  Pallas kernels: 66.1 us -> 68.9 us
    pallas_call x1, Pallas kernels: 63.8 us -> 66.7 us  [on_device(): pl.pallas_call(functools.partial(kernel, elem_count, band_count), out_sha...]
where the time goes in v7:
time: 69.7 us; the launch traced here: 69.6 us
  Pallas kernels  68.9 us (99%)
    pallas_call x1, Pallas kernels, on_device(): pl.pallas_call(functools.partial(kernel, elem_count, band_count), out_sha...  66.7 us
    pallas_call x1, Pallas kernels, on_device(): pl.pallas_call(hand_on, out_shape=tuple((jax.ShapeDtypeStruct(result.shap...  2.26 us

profile of v7, /device:TPU:0, one launch (start us, length us, event | category | flops | bytes accessed | tf_op | source)
XLA Modules:
  0.0 69.6 jit_solution(4146560489281812408)
XLA Ops:
  0.6 66.7 %shard_map.76 = (bf16[8,4,160,128]{3,2,1,0:T(8,128)(2,1)}, f32[40,160]{1,0:T(8,128)}, f32[40,160]{1,0:T(8,128)}) custom-call(s32[4,8]{1,0:T(4,128)} %bitcast.5, s32[6,4,8]{2,1,0:T(4,128)} %bitcast.4, bf16[8,4,160,128]{3,2,1,0:T(8,128)(2,1)} %x_ref.1, bf16[8,4,128,128]{3,2,1,0:T(8,128)(2,1)} %self_ref.1, bf16[8,4,768,128]{3,2,1,0:T(8,128)(2,1)} %bitcast.3), custom_call_target="tpu_custom_call" | custom-call | tf_op jit(solution)/shard_map/pallas_call | solution.py:351
  67.3 2.3 %shard_map.77 = (bf16[8,4,160,128]{3,2,1,0:T(8,128)(2,1)}, f32[40,160]{1,0:T(8,128)}, f32[40,160]{1,0:T(8,128)}) custom-call(bf16[8,4,160,128]{3,2,1,0:T(8,128)(2,1)} %get-tuple-element.6.refs_0_, f32[40,160]{1,0:T(8,128)} %get-tuple-element.7.refs_1_, f32[40,160]{1,0:T(8,128)} %get-tuple-element.8.refs_2_), custom_call_target="tpu_custom_call" | custom-call | tf_op jit(solution)/shard_map/pallas_call | solution.py:376

commit v8 on v5

--- a/solution.py
+++ b/solution.py
@@ -110,10 +110,10 @@
             dst = ext.at[pl.ds(1, rows), pl.ds(landing, length)]
             device = device_at(0, shift)
         elif way == "far":
-            start, landing, length = edge(shift, rows)
-            src = ext.at[pl.ds(start, length), pl.ds(1 + odd * (cols - 1), 1)]
-            dst = ext.at[pl.ds(landing, length), pl.ds((1 - odd) * (cols + 1), 1)]
-            device = device_at(shift, outward)
+            row = 0 if shift < 0 else rows + 1
+            src = ext.at[pl.ds(row, 1), pl.ds(1 + odd * (cols - 1), 1)]
+            dst = ext.at[pl.ds(row, 1), pl.ds((1 - odd) * (cols + 1), 1)]
+            device = device_at(0, outward)
         else:
             row = 0 if shift < 0 else rows + 1
             src = ext.at[pl.ds(row, 1), pl.ds(cols - odd * (cols - 1), 1)]
@@ -131,8 +131,6 @@
     def chosen(*wanted):
         return [index for index, (way, shift) in enumerate(moves) if way in wanted]
 
-    totals[...] = jnp.zeros_like(totals)
-    outgoing[...] = jnp.zeros_like(outgoing)
     for half in range(halves):
         x_loads[half].wait()
         ext = exts[0][half]
@@ -146,8 +144,10 @@
             return carry
 
         lax.fori_loop(0, rows, clear, 0)
-        for which in chosen("vertical", "far", "sideways"):
+        for which in chosen("vertical", "sideways"):
             halo(0, half, which).start()
+    totals[...] = jnp.zeros_like(totals)
+    outgoing[...] = jnp.zeros_like(outgoing)
 
     contract = (((1,), (1,)), ((), ()))
 
@@ -257,7 +257,7 @@
         for half in range(halves):
             for which in chosen("vertical"):
                 halo(step, half, which).wait()
-            for which in chosen("near"):
+            for which in chosen("far", "near"):
                 halo(step, half, which).start()
             for which in chosen("far", "sideways", "near"):
                 halo(step, half, which).wait()
@@ -267,7 +267,7 @@
             for row in (0, rows - 1):
                 update(step, half, [(row, col) for col in range(cols)])
             if step < steps - 1:
-                for which in chosen("vertical", "far"):
+                for which in chosen("vertical"):
                     halo(step + 1, half, which).start()
             inner(step, half, (0, cols - 1))
             if step < steps - 1:

time: 66.9 us -> 88.5 us (1.32)
  Pallas kernels: 66.1 us -> 87.7 us
    pallas_call x1, Pallas kernels: 63.8 us -> 85.4 us  [on_device(): pl.pallas_call(functools.partial(kernel, elem_count, band_count), out_sha...]
where the time goes in v8:
time: 88.5 us; the launch traced here: 88.3 us
  Pallas kernels  87.7 us (99%)
    pallas_call x1, Pallas kernels, on_device(): pl.pallas_call(functools.partial(kernel, elem_count, band_count), out_sha...  85.4 us
    pallas_call x1, Pallas kernels, on_device(): pl.pallas_call(hand_on, out_shape=tuple((jax.ShapeDtypeStruct(result.shap...  2.26 us

profile of v8, /device:TPU:0, one launch (start us, length us, event | category | flops | bytes accessed | tf_op | source)
XLA Modules:
  0.0 88.3 jit_solution(3035503005699779072)
XLA Ops:
  0.6 85.4 %shard_map.76 = (bf16[8,4,160,128]{3,2,1,0:T(8,128)(2,1)}, f32[40,160]{1,0:T(8,128)}, f32[40,160]{1,0:T(8,128)}) custom-call(s32[4,8]{1,0:T(4,128)} %bitcast.5, s32[6,4,8]{2,1,0:T(4,128)} %bitcast.4, bf16[8,4,160,128]{3,2,1,0:T(8,128)(2,1)} %x_ref.1, bf16[8,4,128,128]{3,2,1,0:T(8,128)(2,1)} %self_ref.1, bf16[8,4,768,128]{3,2,1,0:T(8,128)(2,1)} %bitcast.3), custom_call_target="tpu_custom_call" | custom-call | tf_op jit(solution)/shard_map/pallas_call | solution.py:344
  86.1 2.3 %shard_map.77 = (bf16[8,4,160,128]{3,2,1,0:T(8,128)(2,1)}, f32[40,160]{1,0:T(8,128)}, f32[40,160]{1,0:T(8,128)}) custom-call(bf16[8,4,160,128]{3,2,1,0:T(8,128)(2,1)} %get-tuple-element.6.refs_0_, f32[40,160]{1,0:T(8,128)} %get-tuple-element.7.refs_1_, f32[40,160]{1,0:T(8,128)} %get-tuple-element.8.refs_2_), custom_call_target="tpu_custom_call" | custom-call | tf_op jit(solution)/shard_map/pallas_call | solution.py:369
